TPU v7x, 512 devices: a whole 4x8x8 slice. The times are simulated.
512 devices in a mesh: seq: 128 (over y, x_lo, z), chan: 4 (over x_hi, core).
Axes of the slice: x: 4 (x_hi: 2, x_lo: 2; x = x_hi * 2 + x_lo), y: 8, z: 8, core: 2. Of those that a mesh axis runs over, the one named last changes fastest.
Arguments:
- gate_outer: bfloat16 [16384, 2048], P('seq', 'chan'), may hold values from -6 to 6
- gate_inner: bfloat16 [16384, 2048], P('seq', 'chan'), may hold values from -6 to 6
- signal: bfloat16 [16384, 2048], P('seq', 'chan'), may hold values from -6 to 6
- filter_raw: float32 [512, 16384], P('seq'), may hold values from -6 to 6
- cotangent: bfloat16 [16384, 2048], P('seq', 'chan'), may hold values from -6 to 6
Outputs:
- mixed_out: bfloat16 [16384, 2048], P('seq', 'chan')
- grad_outer: bfloat16 [16384, 2048], P('seq', 'chan')
- grad_inner: bfloat16 [16384, 2048], P('seq', 'chan')
- grad_signal: bfloat16 [16384, 2048], P('seq', 'chan')
- grad_filter: float32 [512, 16384], P('seq')
All inputs are finite; a program needn't handle non-finite values.
Results may differ from a plain program's by a relative error of at most 0.0057.
Values may be sent and summed in bfloat16 or wider, within the bound.
No kernel may reach another device: no remote copies, remote signals or barrier semaphores. Data moves between devices by JAX's collectives and lax.ppermute only.
A program may use at most 64 MiB of HBM per device.

v0:
```python
import math

import jax
import jax.numpy as jnp
from jax import lax
from jax.sharding import PartitionSpec as P

HIGHEST_PREC = lax.Precision.HIGHEST


def split_len(padded_len):
    best_rows = 2
    for divisor in range(2, math.isqrt(padded_len) + 1, 2):
        if padded_len % divisor == 0:
            best_rows = divisor
    return (best_rows, padded_len // best_rows)


def dft_tables(padded_len):
    rows_n, cols_n = split_len(padded_len)
    half_rows = rows_n // 2
    row_index = jnp.arange(rows_n, dtype=jnp.int32)
    half_index = jnp.arange(half_rows, dtype=jnp.int32)
    col_index = jnp.arange(cols_n, dtype=jnp.int32)
    angle_one = (row_index[:, None] * half_index[None, :] % rows_n).astype(jnp.float32) * (
        2.0 * math.pi / rows_n
    )
    angle_two = (col_index[:, None] * col_index[None, :] % cols_n).astype(jnp.float32) * (
        2.0 * math.pi / cols_n
    )
    angle_twid = (row_index[:, None] * col_index[None, :] % padded_len).astype(jnp.float32) * (
        2.0 * math.pi / padded_len
    )
    cos_one = jnp.cos(angle_one)
    sin_one = jnp.sin(angle_one)
    cos_two = jnp.cos(angle_two)
    sin_two = jnp.sin(angle_two)
    first_fwd = jnp.stack([cos_one.T, -sin_one.T], axis=1)
    second_fwd = jnp.stack(
        [jnp.stack([cos_two, -sin_two], axis=1), jnp.stack([sin_two, cos_two], axis=1)], axis=0
    )
    second_inv = jnp.stack(
        [jnp.stack([cos_two, sin_two], axis=1), jnp.stack([-sin_two, cos_two], axis=1)], axis=0
    )
    last_inv = jnp.stack([cos_one, -sin_one], axis=0)
    return (
        first_fwd,
        second_fwd,
        second_inv,
        last_inv,
        jnp.cos(angle_twid)[:, :, None],
        jnp.sin(angle_twid)[:, :, None],
    )


def forward_dft(columns, tables_all):
    first_fwd, second_fwd, second_inv, last_inv, twid_cos, twid_sin = tables_all
    blocks = columns.reshape(first_fwd.shape[0], second_fwd.shape[1], columns.shape[1])
    section_a = jnp.einsum("nmb,npk->pkmb", blocks, first_fwd, precision=HIGHEST_PREC)
    real_b = section_a[0] * twid_cos + section_a[1] * twid_sin
    imag_b = section_a[1] * twid_cos - section_a[0] * twid_sin
    section_b = jnp.stack([real_b, imag_b], axis=0)
    return jnp.einsum("pkmb,pmqj->qkjb", section_b, second_fwd, precision=HIGHEST_PREC)


def inverse_dft(spec, tables_all):
    first_fwd, second_fwd, second_inv, last_inv, twid_cos, twid_sin = tables_all
    padded_len = last_inv.shape[1] * second_inv.shape[1]
    section_c = jnp.einsum("pkjb,pjqm->qkmb", spec, second_inv, precision=HIGHEST_PREC)
    real_d = section_c[0] * twid_cos - section_c[1] * twid_sin
    imag_d = section_c[1] * twid_cos + section_c[0] * twid_sin
    section_d = jnp.stack([real_d, imag_d], axis=0)
    result = jnp.einsum("pkmb,pkn->nmb", section_d, last_inv, precision=HIGHEST_PREC)
    return result.reshape(padded_len // 2, spec.shape[3]) * (1.0 / padded_len)


def times_spec(first, second, conj_first):
    if conj_first:
        return jnp.stack(
            [
                first[0] * second[0] + first[1] * second[1],
                first[0] * second[1] - first[1] * second[0],
            ],
            axis=0,
        )
    return jnp.stack(
        [first[0] * second[0] - first[1] * second[1], first[0] * second[1] + first[1] * second[0]],
        axis=0,
    )


def channel_work(inner_cols, grad_cols, filter_rows, groups):
    seq_len, width = inner_cols.shape
    tables_all = dft_tables(2 * seq_len)
    stacked = jnp.concatenate(
        [inner_cols.astype(jnp.float32), grad_cols.astype(jnp.float32), filter_rows.T], axis=1
    )
    spec_all = forward_dft(stacked, tables_all)
    inner_spec = spec_all[..., :width]
    grad_spec = spec_all[..., width : 2 * width]
    tap_spec = jnp.tile(spec_all[..., 2 * width :], (1, 1, 1, groups))
    products = jnp.concatenate(
        [
            times_spec(tap_spec, inner_spec, False),
            times_spec(tap_spec, grad_spec, True),
            times_spec(inner_spec, grad_spec, True),
        ],
        axis=3,
    )
    results = inverse_dft(products, tables_all)
    return (results[:, :width], results[:, width : 2 * width], results[:, 2 * width :])


def body(gate_outer, gate_inner, signal, filter_raw, cotangent):
    tok_rows, chan_cols = gate_outer.shape
    seq_parts = lax.axis_size("seq")
    chan_width = chan_cols // seq_parts
    seq_len = tok_rows * seq_parts
    norm_scale = 1.0 / math.sqrt(seq_len)
    filter_taps = filter_raw * norm_scale
    outer_f = gate_outer.astype(jnp.float32)
    cotan_f = cotangent.astype(jnp.float32)
    inner_prod = (gate_inner.astype(jnp.float32) * signal.astype(jnp.float32)).astype(jnp.bfloat16)
    grad_conv = (cotan_f * outer_f).astype(jnp.bfloat16)
    packed_inner = inner_prod.reshape(1, tok_rows, seq_parts, 1, chan_width)
    packed_grad = grad_conv.reshape(1, tok_rows, seq_parts, 1, chan_width)
    inner_t, grad_t = (
        lax.all_to_all(packed_inner, "seq", split_axis=2, concat_axis=1, tiled=True),
        lax.all_to_all(packed_grad, "seq", split_axis=2, concat_axis=1, tiled=True),
    )
    conv_cols, back_cols, corr_cols = channel_work(
        inner_t.reshape(seq_len, chan_width), grad_t.reshape(seq_len, chan_width), filter_taps, 1
    )
    grad_filter = lax.psum(corr_cols.T * norm_scale, "chan")
    conv_t = conv_cols.astype(jnp.bfloat16).reshape(1, seq_len, 1, 1, chan_width)
    back_t = back_cols.astype(jnp.bfloat16).reshape(1, seq_len, 1, 1, chan_width)
    conv_back, prod_back = (
        lax.all_to_all(conv_t, "seq", split_axis=1, concat_axis=2, tiled=True),
        lax.all_to_all(back_t, "seq", split_axis=1, concat_axis=2, tiled=True),
    )
    conv_f = conv_back.reshape(tok_rows, chan_cols).astype(jnp.float32)
    prod_f = prod_back.reshape(tok_rows, chan_cols).astype(jnp.float32)
    mixed_out = (outer_f * conv_f).astype(jnp.bfloat16)
    grad_outer = (cotan_f * conv_f).astype(jnp.bfloat16)
    grad_inner = (prod_f * signal.astype(jnp.float32)).astype(jnp.bfloat16)
    grad_signal = (prod_f * gate_inner.astype(jnp.float32)).astype(jnp.bfloat16)
    return (mixed_out, grad_outer, grad_inner, grad_signal, grad_filter)


def solution(mesh):
    in_specs = (
        P("seq", "chan"),
        P("seq", "chan"),
        P("seq", "chan"),
        P("seq", None),
        P("seq", "chan"),
    )
    out_specs = (
        P("seq", "chan"),
        P("seq", "chan"),
        P("seq", "chan"),
        P("seq", "chan"),
        P("seq", None),
    )
    return jax.shard_map(body, mesh=mesh, in_specs=in_specs, out_specs=out_specs, check_vma=False)
```

profile of v0, /device:TPU:1, one launch (start us, length us, event | category | flops | bytes accessed | tf_op | source)
XLA Modules:
  0.0 407.1 jit_solution(10686408543051850736)
XLA Ops:
  7.2 1.1 copy.77
  8.3 1.0 copy.82
  9.3 0.7 fusion.38
  10.0 19.3 %all-to-all-start.1 = ((bf16[1,128,128,1,4]{1,4,3,0,2:T(4,128)(2,1)}), bf16[1,128,128,1,4]{1,4,3,0,2:T(4,128)(2,1)S(1)}, u32[]{:S(2)}, u32[]{:S(2)}) async-start(bf16[1,128,128,1,4]{1,4,3,0,2:T(4,128)(2,1)} %bitcast.17), calls=%async_computation.1 | async-start | bytes 262144 | tf_op jit(solution)/shard_map/all_to_all | solution.py:129
  29.3 0.1 sine_negate_fusion.1
  29.4 1.0 fusion.55
  30.4 0.5 fusion.62
  30.9 1.0 fusion.52
  32.0 1.0 multiply_bitcast_fusion
  33.0 1.0 fusion.32
  34.0 0.1 sine_negate_fusion
  34.3 0.1 copy.80
  34.4 0.7 fusion.36
  35.1 6.1 %all-to-all-done.1 = bf16[1,128,128,1,4]{1,4,3,0,2:T(4,128)(2,1)S(1)} async-done(((bf16[1,128,128,1,4]{1,4,3,0,2:T(4,128)(2,1)}), bf16[1,128,128,1,4]{1,4,3,0,2:T(4,128)(2,1)S(1)}, u32[]{:S(2)}, u32[]{:S(2)}) %all-to-all-start.1) | async-done | bytes 131104 | tf_op jit(solution)/shard_map/all_to_all | solution.py:129
  41.2 8.3 %all-to-all-start = ((bf16[1,128,128,1,4]{1,4,3,0,2:T(4,128)(2,1)}), bf16[1,128,128,1,4]{1,4,3,0,2:T(4,128)(2,1)S(1)}, u32[]{:S(2)}, u32[]{:S(2)}) async-start(bf16[1,128,128,1,4]{1,4,3,0,2:T(4,128)(2,1)} %bitcast.12), calls=%async_computation | async-start | bytes 262144 | tf_op jit(solution)/shard_map/all_to_all | solution.py:128
  49.5 11.6 %all-to-all-done = bf16[1,128,128,1,4]{1,4,3,0,2:T(4,128)(2,1)S(1)} async-done(((bf16[1,128,128,1,4]{1,4,3,0,2:T(4,128)(2,1)}), bf16[1,128,128,1,4]{1,4,3,0,2:T(4,128)(2,1)S(1)}, u32[]{:S(2)}, u32[]{:S(2)}) %all-to-all-start) | async-done | bytes 131104 | tf_op jit(solution)/shard_map/all_to_all | solution.py:128
  61.2 0.2 pad_maximum_fusion.1
  61.4 0.3 copy.109
  61.7 2.7 fusion.27
  64.4 0.4 multiply_add_fusion.1
  64.8 0.6 copy-done
  65.4 5.4 %fusion.9 = f32[2,128,256,12]{1,2,3,0:T(8,128)S(1)} fusion(f32[1,256,2,256]{1,3,0,2:T(8,128)S(1)} %get-tuple-element.38, f32[1,256,2,256]{1,3,0,2:T(8,128)S(1)} %copy-done, f32[1,128,256,12]{2,1,3,0:T(8,128)S(1)} %get-tuple-element.28, f32[1,128,256,12]{2,1,3,0:T(8,128)S(1)} %get-tuple-element.27), kind=kOutput, calls=%fused_computation.11 | convolution fusion | flops 4832886784 | bytes 7340032 | tf_op jit(solution)/shard_map/pkmb,pmqj->qkjb/dot_general | solution.py:63
  70.9 0.2 multiply_subtract_fusion.4
  71.2 5.8 %fusion.12 = f32[2,128,256,12]{2,1,3,0:T(8,128)S(1)} fusion(f32[1,128,256,4]{1,2,3,0:T(8,128)S(1)} %get-tuple-element.34, f32[1,128,256,4]{1,2,3,0:T(8,128)S(1)} %get-tuple-element.33, f32[1,128,256,4]{1,2,3,0:T(8,128)S(1)} %get-tuple-element.31, f32[1,128,256,4]{1,2,3,0:T(8,128)S(1)} %get-tuple-element.30, f32[1,128,256,4]{1,2,3,0:T(8,128)S(1)} %get-tuple-element.32, ...), kind=kOutput, calls=%fused_computation.12 | convolution fusion | flops 4836032512 | bytes 7340032 | tf_op jit(solution)/shard_map/pkjb,pjqm->qkmb/dot_general | solution.py:69
  77.0 0.4 multiply_subtract_fusion
  77.4 2.0 fusion.21
  79.5 0.6 copy.110
  80.3 12.9 %copy.91 = bf16[1,16384,1,1,4]{4,3,2,0,1:T(2,128)(2,1)} copy(bf16[1,16384,1,1,4]{1,4,3,2,0:T(4,128)(2,1)S(1)} %get-tuple-element.35) | data formatting | bytes 262144 | tf_op jit(solution)/shard_map/reshape | solution.py:136
  93.2 0.5 broadcast.374
  93.7 90.8 %reduce.1 = bf16[16384,4]{1,0:T(8,128)(2,1)} reduce(bf16[16384,1,1,1,4]{4,3,2,1,0:T(2,128)(2,1)} %bitcast.113, bf16[]{:T(256)} %broadcast.374), dimensions={1,2,3}, to_apply=%bitcast.104.reduce_sub_computation | reduce | bytes 262146
  184.5 9.4 %reshape.329 = bf16[128,2,256]{2,1,0:T(2,128)(2,1)} reshape(bf16[16384,4]{1,0:T(8,128)(2,1)} %reduce.1) | data formatting | bytes 262144
  193.9 6.2 %all-to-all-start.3 = ((bf16[128,2,256]{2,1,0:T(2,128)(2,1)}), bf16[128,2,256]{2,1,0:T(2,128)(2,1)S(1)}, u32[]{:S(2)}, u32[]{:S(2)}) async-start(bf16[128,2,256]{2,1,0:T(2,128)(2,1)} %reshape.329), calls=%async_computation.3 | async-start | bytes 262144 | tf_op jit(solution)/shard_map/all_to_all | solution.py:139
  200.2 0.7 fusion.43
  200.9 12.9 %copy.89 = bf16[1,16384,1,1,4]{4,3,2,0,1:T(2,128)(2,1)} copy(bf16[1,16384,1,1,4]{1,4,3,2,0:T(4,128)(2,1)S(1)} %get-tuple-element.36) | data formatting | bytes 262144 | tf_op jit(solution)/shard_map/reshape | solution.py:135
  213.8 90.8 %reduce = bf16[16384,4]{1,0:T(8,128)(2,1)} reduce(bf16[16384,1,1,1,4]{4,3,2,1,0:T(2,128)(2,1)} %bitcast.114, bf16[]{:T(256)} %broadcast.374), dimensions={1,2,3}, to_apply=%bitcast.102.reduce_sub_computation | reduce | bytes 262146
  304.6 9.3 %reshape.327 = bf16[128,2,256]{2,1,0:T(2,128)(2,1)} reshape(bf16[16384,4]{1,0:T(8,128)(2,1)} %reduce) | data formatting | bytes 262144
  313.9 14.3 %all-to-all-start.2 = ((bf16[128,2,256]{2,1,0:T(2,128)(2,1)}), bf16[128,2,256]{2,1,0:T(2,128)(2,1)S(1)}, u32[]{:S(2)}, u32[]{:S(2)}) async-start(bf16[128,2,256]{2,1,0:T(2,128)(2,1)} %reshape.327), calls=%async_computation.2 | async-start | bytes 262144 | tf_op jit(solution)/shard_map/all_to_all | solution.py:138
  328.2 17.1 %reshape.330 = bf16[16384,1,1,1,4]{4,3,2,1,0:T(2,128)(2,1)} reshape(bf16[128,2,256]{2,1,0:T(2,128)(2,1)S(1)} %all-to-all-done.3) | data formatting | bytes 262144
  345.3 10.8 %bitcast_convert_fusion = f32[1,16384,1,1,4]{4,3,2,0,1:T(1,128)} fusion(bf16[16384,1,1,1,4]{4,3,2,1,0:T(2,128)(2,1)} %reshape.330), kind=kLoop, calls=%fused_computation.117 | loop fusion | flops 65536 | bytes 393216 | tf_op jit(solution)/shard_map/convert_element_type | solution.py:142
  356.2 5.5 %copy.92 = f32[1,128,128,1,1,4]{2,5,1,4,3,0:T(4,128)S(1)} copy(f32[1,128,128,1,1,4]{5,2,1,4,3,0:T(8,128)} %bitcast.115) | data formatting | bytes 524288 | tf_op jit(solution)/shard_map/convert_element_type | solution.py:142
  361.7 17.1 %reshape.328 = bf16[16384,1,1,1,4]{4,3,2,1,0:T(2,128)(2,1)} reshape(bf16[128,2,256]{2,1,0:T(2,128)(2,1)S(1)} %all-to-all-done.2) | data formatting | bytes 262144
  378.8 10.8 %bitcast_convert_fusion.1 = f32[1,16384,1,1,4]{4,3,2,0,1:T(1,128)} fusion(bf16[16384,1,1,1,4]{4,3,2,1,0:T(2,128)(2,1)} %reshape.328), kind=kLoop, calls=%fused_computation.118 | loop fusion | flops 65536 | bytes 393216 | tf_op jit(solution)/shard_map/convert_element_type | solution.py:141
  389.7 0.8 copy.96
  390.5 0.8 copy.95
  391.2 5.5 %copy.90 = f32[1,128,128,1,1,4]{2,5,1,4,3,0:T(4,128)S(1)} copy(f32[1,128,128,1,1,4]{5,2,1,4,3,0:T(8,128)} %bitcast.112) | data formatting | bytes 524288 | tf_op jit(solution)/shard_map/convert_element_type | solution.py:141
  396.8 0.8 copy.94
  397.6 0.8 copy.93
  398.3 1.7 copy.124
  (19 shorter events, 0.7 us)
Async XLA Ops:
  7.2 27.0 %copy-start.1 = (bf16[128,512]{1,0:T(8,128)(2,1)S(1)}, bf16[128,512]{1,0:T(8,128)(2,1)}, u32[]{:S(2)}) copy-start(bf16[128,512]{1,0:T(8,128)(2,1)} %param.6) | copy-start | bytes 393220
  7.2 27.1 %copy-start.2 = (bf16[128,512]{1,0:T(8,128)(2,1)S(1)}, bf16[128,512]{1,0:T(8,128)(2,1)}, u32[]{:S(2)}) copy-start(bf16[128,512]{1,0:T(8,128)(2,1)} %param.7) | copy-start | bytes 393220
  10.0 31.2 %all-to-all-start.1 = ((bf16[1,128,128,1,4]{1,4,3,0,2:T(4,128)(2,1)}), bf16[1,128,128,1,4]{1,4,3,0,2:T(4,128)(2,1)S(1)}, u32[]{:S(2)}, u32[]{:S(2)}) async-start(bf16[1,128,128,1,4]{1,4,3,0,2:T(4,128)(2,1)} %bitcast.17), calls=%async_computation.1 | async-start | bytes 262144 | tf_op jit(solution)/shard_map/all_to_all | solution.py:129
  41.2 20.0 %all-to-all-start = ((bf16[1,128,128,1,4]{1,4,3,0,2:T(4,128)(2,1)}), bf16[1,128,128,1,4]{1,4,3,0,2:T(4,128)(2,1)S(1)}, u32[]{:S(2)}, u32[]{:S(2)}) async-start(bf16[1,128,128,1,4]{1,4,3,0,2:T(4,128)(2,1)} %bitcast.12), calls=%async_computation | async-start | bytes 262144 | tf_op jit(solution)/shard_map/all_to_all | solution.py:128
  64.4 1.0 copy-start
  193.9 120.0 %all-to-all-start.3 = ((bf16[128,2,256]{2,1,0:T(2,128)(2,1)}), bf16[128,2,256]{2,1,0:T(2,128)(2,1)S(1)}, u32[]{:S(2)}, u32[]{:S(2)}) async-start(bf16[128,2,256]{2,1,0:T(2,128)(2,1)} %reshape.329), calls=%async_computation.3 | async-start | bytes 262144 | tf_op jit(solution)/shard_map/all_to_all | solution.py:139
  200.1 198.2 %all-reduce.2.cloned.1.call-start = ((), (), s32[]{:S(2)}) async-start(), calls=%async_computation.4 | async-start | bytes 524288 | tf_op jit(solution)/shard_map/psum | solution.py:134
  313.9 47.8 %all-to-all-start.2 = ((bf16[128,2,256]{2,1,0:T(2,128)(2,1)}), bf16[128,2,256]{2,1,0:T(2,128)(2,1)S(1)}, u32[]{:S(2)}, u32[]{:S(2)}) async-start(bf16[128,2,256]{2,1,0:T(2,128)(2,1)} %reshape.327), calls=%async_computation.2 | async-start | bytes 262144 | tf_op jit(solution)/shard_map/all_to_all | solution.py:138
Sparse Core Ops, SparseCore 0:
  204.4 54.0 all-reduce.1
where the time goes:
time: 415 us; the launch traced here: 407 us
  other arithmetic  212 us (51%)
  local copies, waits for them, and re-layouts  99 us (24%)
  starting transfers between devices  48.1 us (12%)
  waiting for transfers between devices  17.7 us (4%)
  matrix products  15.9 us (4%)
  between operations  14.5 us (3%)
    unnamed x2, other arithmetic  182 us
    unnamed x23, local copies, waits for them, and re-layouts  62.1 us
    all_to_all x1, starting transfers between devices, body(): lax.all_to_all(packed_grad, 'seq', split_axis=2, concat_axis=1, tiled=True)  19.3 us
    all_to_all x1, starting transfers between devices, body(): lax.all_to_all(conv_t, 'seq', split_axis=1, concat_axis=2, tiled=True)  14.3 us
    reshape x2, local copies, waits for them, and re-layouts, body(): back_cols.astype(jnp.bfloat16).reshape(1, seq_len, 1, 1, chan_width)  13 us
    reshape x1, local copies, waits for them, and re-layouts, body(): conv_cols.astype(jnp.bfloat16).reshape(1, seq_len, 1, 1, chan_width)  12.9 us
    all_to_all x1, waiting for transfers between devices, body(): lax.all_to_all(packed_inner, 'seq', split_axis=2, concat_axis=1, tiled=True)  11.6 us
    convert_element_type x1, other arithmetic, body(): prod_f = prod_back.reshape(tok_rows, chan_cols).astype(jnp.float32)  10.8 us
  transfers between devices with their start and end apart: 5, of which 2 were waited for; matrix products, arithmetic and copies ran while one was open for 47% of the time, Pallas kernels for 0%

commit v1 on v0

v1 whole, which is shorter than its diff:
```python
import math

import jax
import jax.numpy as jnp
import numpy as np
import ml_dtypes
from jax import lax
from jax.experimental import pallas as pl
from jax.experimental.pallas import tpu as pltpu
from jax.sharding import PartitionSpec as P

BF = jnp.bfloat16
F32 = jnp.float32
VMEM_BYTES = 40 * 1024 * 1024


def split_np(table):
    high = table.astype(ml_dtypes.bfloat16)
    low = (table - high.astype(np.float64)).astype(ml_dtypes.bfloat16)
    return high, low


def dft_tables(rows_n, cols_n, scale):
    length = rows_n * cols_n
    row_i = np.arange(rows_n, dtype=np.float64)
    col_i = np.arange(cols_n, dtype=np.float64)
    ang_one = -2.0 * np.pi * np.outer(row_i + 0.25, row_i) / rows_n
    ang_twid = -2.0 * np.pi * np.outer(row_i + 0.25, col_i) / length
    ang_two = 2.0 * np.pi * (np.outer(col_i, col_i) % cols_n) / cols_n
    first = np.concatenate([np.cos(ang_one), np.sin(ang_one)], axis=0)
    cos_two, sin_two = np.cos(ang_two), np.sin(ang_two)
    second = np.block([[cos_two, -sin_two], [sin_two, cos_two]])
    second_inv = second.T
    last = first.T * scale
    first_h, first_l = split_np(first)
    second_h, second_l = split_np(second)
    inv_h, inv_l = split_np(second_inv)
    last_h, last_l = split_np(last)
    return dict(
        first=np.concatenate([first_h, first_l], axis=1),
        twid=np.concatenate([np.cos(ang_twid), -np.sin(ang_twid)], axis=1).astype(np.float32),
        second=np.concatenate([second_h, second_h, second_l], axis=0),
        inverse=np.concatenate([inv_h, inv_h, inv_l], axis=0),
        last=np.concatenate([last_h, last_l, last_h], axis=1),
    )


def split_hl(value):
    high = value.astype(BF)
    low = (value - high.astype(F32)).astype(BF)
    return high, low


def dot32(left, right):
    return lax.dot_general(left, right, (((1,), (0,)), ((), ())), preferred_element_type=F32)


def pack_kernel(outer_ref, inner_ref, signal_ref, cotan_ref, out_ref, flat_ref, mix_ref):
    prod = (inner_ref[...].astype(F32) * signal_ref[...].astype(F32)).astype(BF).astype(F32)
    grad = (cotan_ref[...].astype(F32) * outer_ref[...].astype(F32)).astype(BF).astype(F32)
    count = out_ref.shape[0] // 8
    for half, value in enumerate((prod, grad)):
        flat_ref[half] = value.T
        for c in range(4):
            mix_ref[pl.ds(4 * half + c, count, stride=8), :] = flat_ref[
                half, pl.ds(c, count, stride=4), :
            ]
    out_ref[...] = mix_ref[...].astype(BF)


def second_stage(part, twid_cos, twid_sin, second):
    rows = twid_cos.shape[0]
    pieces = []
    for one in part:
        real, imag = one[:rows], one[rows:]
        turned = jnp.concatenate(
            [real * twid_cos + imag * twid_sin, imag * twid_cos - real * twid_sin], axis=1
        )
        high, low = split_hl(turned)
        pieces.append(jnp.concatenate([high, low, high], axis=1))
    return dot32(jnp.concatenate(pieces, axis=0), second)


def filter_kernel(filt_ref, first_ref, twid_ref, second_ref, out_ref, rows_ref):
    rows = twid_ref.shape[0]
    cols = twid_ref.shape[1] // 2
    for n in range(rows):
        rows_ref[pl.ds(4 * n, 4), :] = filt_ref[:, cols * n : cols * (n + 1)]
    first = first_ref[...]
    parts = []
    for f in range(4):
        high, low = split_hl(rows_ref[pl.ds(f, rows, stride=4), :])
        parts.append((high, low))
    high = jnp.concatenate([h for h, _ in parts], axis=1)
    low = jnp.concatenate([l for _, l in parts], axis=1)
    stage = dot32(first, jnp.concatenate([high, high], axis=0)) + dot32(first[:, :rows], low)
    out_ref[...] = second_stage(
        [stage[:, cols * f : cols * (f + 1)] for f in range(4)],
        twid_ref[:, :cols],
        twid_ref[:, cols:],
        second_ref[...],
    )


def conv_kernel(
    recv_ref, spec_ref, first_ref, twid_ref, second_ref, inverse_ref, last_ref,
    send_ref, corr_ref, flat_ref, back_ref, corr_mix_ref,
):
    rows = twid_ref.shape[0]
    cols = twid_ref.shape[1] // 2
    twid_cos, twid_sin = twid_ref[:, :cols], twid_ref[:, cols:]
    flat_ref[...] = recv_ref[...].astype(F32)
    columns = jnp.concatenate(
        [flat_ref[pl.ds(c, rows, stride=8), :].astype(BF) for c in range(8)], axis=1
    )
    stage = dot32(first_ref[...], jnp.concatenate([columns, columns], axis=0))
    spec = second_stage(
        [stage[:, cols * c : cols * (c + 1)] for c in range(8)],
        twid_cos, twid_sin, second_ref[...],
    )

    def parts_of(array, c):
        block = array[rows * c : rows * (c + 1)]
        return block[:, :cols], block[:, cols:]

    products = []
    for c in range(4):
        tap_r, tap_i = spec_ref[rows * c : rows * (c + 1), :cols], spec_ref[rows * c : rows * (c + 1), cols:]
        in_r, in_i = parts_of(spec, c)
        gr_r, gr_i = parts_of(spec, 4 + c)
        products.append((4 * 0 + c, tap_r * in_r - tap_i * in_i, tap_r * in_i + tap_i * in_r))
        products.append((4 * 1 + c, tap_r * gr_r + tap_i * gr_i, tap_r * gr_i - tap_i * gr_r))
        products.append((4 * 2 + c, in_r * gr_r + in_i * gr_i, in_r * gr_i - in_i * gr_r))
    products.sort(key=lambda item: item[0])
    pieces = []
    for _, real, imag in products:
        high, low = split_hl(jnp.concatenate([real, imag], axis=1))
        pieces.append(jnp.concatenate([high, low, high], axis=1))
    turned = dot32(jnp.concatenate(pieces, axis=0), inverse_ref[...])
    columns = []
    for c in range(12):
        real, imag = parts_of(turned, c)
        value = jnp.concatenate(
            [real * twid_cos - imag * twid_sin, imag * twid_cos + real * twid_sin], axis=0
        )
        high, low = split_hl(value)
        columns.append(jnp.concatenate([high, high, low], axis=0))
    result = dot32(last_ref[...], jnp.concatenate(columns, axis=1))
    for c in range(8):
        back_ref[pl.ds(c, rows, stride=8), :] = result[:, cols * c : cols * (c + 1)]
    send_ref[...] = back_ref[...].astype(BF)
    for c in range(4):
        corr_mix_ref[pl.ds(c, rows, stride=4), :] = result[:, cols * (8 + c) : cols * (9 + c)]
    corr_ref[...] = corr_mix_ref[...].astype(corr_ref.dtype)


def gate_kernel(
    recv_ref, outer_ref, inner_ref, signal_ref, cotan_ref,
    mixed_ref, gouter_ref, ginner_ref, gsignal_ref, flat_ref, mix_ref,
):
    count = recv_ref.shape[0] // 8
    flat_ref[...] = recv_ref[...].astype(F32)
    for c in range(8):
        mix_ref[c // 4, pl.ds(c % 4, count, stride=4), :] = flat_ref[pl.ds(c, count, stride=8), :]
    conv = mix_ref[0].T
    prod = mix_ref[1].T
    mixed_ref[...] = (outer_ref[...].astype(F32) * conv).astype(BF)
    gouter_ref[...] = (cotan_ref[...].astype(F32) * conv).astype(BF)
    ginner_ref[...] = (prod * signal_ref[...].astype(F32)).astype(BF)
    gsignal_ref[...] = (prod * inner_ref[...].astype(F32)).astype(BF)


def sum_kernel(part_ref, out_ref):
    rows = part_ref.shape[1] // 4
    total = part_ref[0].astype(F32)
    for g in range(1, part_ref.shape[0]):
        total = total + part_ref[g].astype(F32)
    for n in range(rows):
        out_ref[:, 128 * n : 128 * (n + 1)] = total[4 * n : 4 * n + 4, :]


def call(kernel, out_shape, scratch, flops=0, nbytes=0):
    return pl.pallas_call(
        kernel,
        out_shape=out_shape,
        scratch_shapes=scratch,
        compiler_params=pltpu.CompilerParams(vmem_limit_bytes=VMEM_BYTES),
        cost_estimate=pl.CostEstimate(flops=flops, bytes_accessed=nbytes, transcendentals=0),
    )


def body(gate_outer, gate_inner, signal, filter_raw, cotangent):
    tok_rows, chan_cols = gate_outer.shape
    seq_parts = lax.axis_size("seq")
    rows, cols = seq_parts, tok_rows
    seq_len = rows * cols
    tables = dft_tables(rows, cols, 1.0 / math.sqrt(seq_len) / seq_len)
    first, twid = jnp.asarray(tables["first"]), jnp.asarray(tables["twid"])
    second, inverse = jnp.asarray(tables["second"]), jnp.asarray(tables["inverse"])
    last = jnp.asarray(tables["last"])
    wide = 8 * rows
    packed = call(
        pack_kernel,
        jax.ShapeDtypeStruct((wide, cols), BF),
        [pltpu.VMEM((2, chan_cols, tok_rows), F32), pltpu.VMEM((wide, cols), F32)],
        nbytes=6 * 2 * tok_rows * chan_cols,
    )(gate_outer, gate_inner, signal, cotangent)
    received = lax.all_to_all(packed.reshape(rows, 8, cols), "seq", 0, 0, tiled=True)
    tap_spec = call(
        filter_kernel,
        jax.ShapeDtypeStruct((4 * rows, 2 * cols), F32),
        [pltpu.VMEM((4 * rows, cols), F32)],
        flops=10**9, nbytes=10**6,
    )(filter_raw, first, twid, second)
    send, corr = call(
        conv_kernel,
        (
            jax.ShapeDtypeStruct((wide, cols), BF),
            jax.ShapeDtypeStruct((4 * rows, cols), BF),
        ),
        [
            pltpu.VMEM((wide, cols), F32),
            pltpu.VMEM((wide, cols), F32),
            pltpu.VMEM((4 * rows, cols), F32),
        ],
        flops=3 * 10**9, nbytes=2 * 10**6,
    )(received.reshape(wide, cols), tap_spec, first, twid, second, inverse, last)
    parts = lax.all_gather(corr, "chan", axis=0, tiled=False)
    returned = lax.all_to_all(send.reshape(rows, 8, cols), "seq", 0, 0, tiled=True)
    grad_filter = call(
        sum_kernel,
        jax.ShapeDtypeStruct(filter_raw.shape, F32),
        [],
        nbytes=10**6,
    )(parts)
    outs = call(
        gate_kernel,
        tuple(jax.ShapeDtypeStruct((tok_rows, chan_cols), BF) for _ in range(4)),
        [pltpu.VMEM((wide, cols), F32), pltpu.VMEM((2, chan_cols, tok_rows), F32)],
        nbytes=10 * 2 * tok_rows * chan_cols,
    )(returned.reshape(wide, cols), gate_outer, gate_inner, signal, cotangent)
    return (*outs, grad_filter)


def solution(mesh):
    in_specs = (
        P("seq", "chan"),
        P("seq", "chan"),
        P("seq", "chan"),
        P("seq", None),
        P("seq", "chan"),
    )
    out_specs = (
        P("seq", "chan"),
        P("seq", "chan"),
        P("seq", "chan"),
        P("seq", "chan"),
        P("seq", None),
    )
    return jax.shard_map(body, mesh=mesh, in_specs=in_specs, out_specs=out_specs, check_vma=False)
```

time: 415 us -> 64.2 us (0.15)
  the two profiles are of different devices: /device:TPU:1 before, /device:TPU:4 now
where the time goes in v1:
time: 64.2 us; the launch traced here: 63.9 us
  starting transfers between devices  24.7 us (38%)
  waiting for transfers between devices  19.2 us (30%)
  blocking collectives  8.96 us (14%)
  Pallas kernels  6.62 us (10%)
  local copies, waits for them, and re-layouts  3.65 us (6%)
  between operations  0.73 us (1%)
    all_to_all x1, starting transfers between devices, body(): lax.all_to_all(packed.reshape(rows, 8, cols), 'seq', 0, 0, tiled=True)  18.6 us
    all_to_all x1, waiting for transfers between devices, body(): lax.all_to_all(packed.reshape(rows, 8, cols), 'seq', 0, 0, tiled=True)  14.6 us
    all_gather x1, blocking collectives, body(): parts = lax.all_gather(corr, 'chan', axis=0, tiled=False)  8.96 us
    all_to_all x1, starting transfers between devices, body(): lax.all_to_all(send.reshape(rows, 8, cols), 'seq', 0, 0, tiled=True)  6.16 us
    all_to_all x1, waiting for transfers between devices, body(): lax.all_to_all(send.reshape(rows, 8, cols), 'seq', 0, 0, tiled=True)  4.53 us
    unnamed x28, local copies, waits for them, and re-layouts  3.65 us
    pallas_call x1, Pallas kernels, body(): call(conv_kernel, (jax.ShapeDtypeStruct((wide, cols), BF), jax.ShapeDtype...  3.26 us
  transfers between devices with their start and end apart: 2, of which 2 were waited for; matrix products, arithmetic and copies ran while one was open for 0% of the time, Pallas kernels for 2%

profile of v1, /device:TPU:4, one launch (start us, length us, event | category | flops | bytes accessed | tf_op | source)
XLA Modules:
  0.0 63.9 jit_solution(3292096290663424648)
XLA Ops:
  0.6 0.0 copy-start
  0.6 0.9 %copy-done = bf16[128,512]{1,0:T(8,128)(2,1)S(1)} copy-done((bf16[128,512]{1,0:T(8,128)(2,1)S(1)}, bf16[128,512]{1,0:T(8,128)(2,1)}, u32[]{:S(2)}) %copy-start) | copy-done | bytes 131096
  1.5 0.0 copy-start.2
  1.5 0.9 %copy-done.2 = bf16[128,512]{1,0:T(8,128)(2,1)S(1)} copy-done((bf16[128,512]{1,0:T(8,128)(2,1)S(1)}, bf16[128,512]{1,0:T(8,128)(2,1)}, u32[]{:S(2)}) %copy-start.2) | copy-done | bytes 131096
  2.4 0.0 copy-start.4
  2.4 0.9 %copy-done.4 = bf16[128,512]{1,0:T(8,128)(2,1)S(1)} copy-done((bf16[128,512]{1,0:T(8,128)(2,1)S(1)}, bf16[128,512]{1,0:T(8,128)(2,1)}, u32[]{:S(2)}) %copy-start.4) | copy-done | bytes 131096
  3.3 0.0 copy-start.6
  3.3 0.9 %copy-done.6 = bf16[128,512]{1,0:T(8,128)(2,1)S(1)} copy-done((bf16[128,512]{1,0:T(8,128)(2,1)S(1)}, bf16[128,512]{1,0:T(8,128)(2,1)}, u32[]{:S(2)}) %copy-start.6) | copy-done | bytes 131096
  4.3 0.0 copy-start.9
  4.3 0.9 %shard_map.137 = bf16[1024,128]{1,0:T(8,128)(2,1)} custom-call(bf16[128,512]{1,0:T(8,128)(2,1)S(1)} %copy-done, bf16[128,512]{1,0:T(8,128)(2,1)S(1)} %copy-done.2, bf16[128,512]{1,0:T(8,128)(2,1)S(1)} %copy-done.4, bf16[128,512]{1,0:T(8,128)(2,1)S(1)} %copy-done.6), custom_call_target="tpu_custom_call" | custom-call | bytes 786432 | tf_op jit(solution)/shard_map/pallas_call | solution.py:202
  5.2 0.0 copy-start.8
  5.2 0.0 copy-start.12
  5.2 0.0 copy-start.13
  5.2 18.6 %all-to-all-start = ((bf16[128,8,128]{2,1,0:T(8,128)(2,1)}), bf16[128,8,128]{2,1,0:T(8,128)(2,1)S(1)}, u32[]{:S(2)}, u32[]{:S(2)}) async-start(bf16[128,8,128]{2,1,0:T(8,128)(2,1)} %bitcast), calls=%async_computation | async-start | bytes 524288 | tf_op jit(solution)/shard_map/all_to_all | solution.py:208
  23.8 0.0 copy-done.9
  23.8 0.0 copy-done.8
  23.8 0.0 copy-done.12
  23.8 0.0 copy-done.13
  23.8 0.0 copy-start.10
  23.8 0.0 copy-start.11
  23.8 0.7 %shard_map.138.spec_ref = f32[512,256]{1,0:T(8,128)S(1)} custom-call(f32[4,16384]{1,0:T(4,128)S(1)} %copy-done.8, bf16[256,256]{1,0:T(8,128)(2,1)S(1)} %copy-done.13, f32[128,256]{1,0:T(8,128)S(1)} %copy-done.12, bf16[768,256]{1,0:T(8,128)(2,1)S(1)} %copy-done.9), custom_call_target="tpu_custom_call" | custom-call | flops 1000000000 | bytes 1000000 | tf_op jit(solution)/shard_map/pallas_call | solution.py:209
  24.5 14.6 %all-to-all-done = bf16[128,8,128]{2,1,0:T(8,128)(2,1)S(1)} async-done(((bf16[128,8,128]{2,1,0:T(8,128)(2,1)}), bf16[128,8,128]{2,1,0:T(8,128)(2,1)S(1)}, u32[]{:S(2)}, u32[]{:S(2)}) %all-to-all-start) | async-done | bytes 262176 | tf_op jit(solution)/shard_map/all_to_all | solution.py:208
  39.2 0.0 copy-done.10
  39.2 0.0 copy-done.11
  39.2 3.3 %shard_map.139 = (bf16[1024,128]{1,0:T(8,128)(2,1)}, bf16[512,128]{1,0:T(8,128)(2,1)S(1)}) custom-call(bf16[1024,128]{1,0:T(8,128)(2,1)S(1)} %bitcast.7, f32[512,256]{1,0:T(8,128)S(1)} %shard_map.138.spec_ref, bf16[256,256]{1,0:T(8,128)(2,1)S(1)} %copy-done.13, f32[128,256]{1,0:T(8,128)S(1)} %copy-done.12, bf16[768,256]{1,0:T(8,128)(2,1)S(1)} %copy-done.9, ...), custom_call_target="tpu_custom_call" | custom-call | flops 3000000000 | bytes 2000000 | tf_op jit(solution)/shard_map/pallas_call | solution.py:215
  42.4 6.2 %all-to-all-start.1 = ((bf16[128,8,128]{2,1,0:T(8,128)(2,1)}), bf16[128,8,128]{2,1,0:T(8,128)(2,1)S(1)}, u32[]{:S(2)}, u32[]{:S(2)}) async-start(bf16[128,8,128]{2,1,0:T(8,128)(2,1)} %bitcast.2), calls=%async_computation.1 | async-start | bytes 524288 | tf_op jit(solution)/shard_map/all_to_all | solution.py:229
  48.6 9.0 %all-gather = bf16[2048,128]{1,0:T(8,128)(2,1)S(1)} all-gather(bf16[512,128]{1,0:T(8,128)(2,1)S(1)} %get-tuple-element.16), channel_id=2, replica_groups=mesh['seq'=128,'chan'=4] {'chan'}, dimensions={0}, use_global_device_ids=true | all-gather | bytes 655360 | tf_op jit(solution)/shard_map/all_gather | solution.py:228
  57.6 0.0 copy-start.1
  57.6 0.0 copy-start.3
  57.6 0.0 copy-start.5
  57.6 0.0 copy-start.7
  57.6 0.8 %shard_map.141 = f32[4,16384]{1,0:T(4,128)} custom-call(bf16[4,512,128]{2,1,0:T(8,128)(2,1)S(1)} %bitcast.5), custom_call_target="tpu_custom_call" | custom-call | bytes 1000000 | tf_op jit(solution)/shard_map/pallas_call | solution.py:230
  58.3 4.5 %all-to-all-done.1 = bf16[128,8,128]{2,1,0:T(8,128)(2,1)S(1)} async-done(((bf16[128,8,128]{2,1,0:T(8,128)(2,1)}), bf16[128,8,128]{2,1,0:T(8,128)(2,1)S(1)}, u32[]{:S(2)}, u32[]{:S(2)}) %all-to-all-start.1) | async-done | bytes 262176 | tf_op jit(solution)/shard_map/all_to_all | solution.py:229
  62.9 0.0 copy-done.1
  62.9 0.0 copy-done.3
  62.9 0.0 copy-done.5
  62.9 0.0 copy-done.7
  62.9 1.0 %shard_map.140 = (bf16[128,512]{1,0:T(8,128)(2,1)}, bf16[128,512]{1,0:T(8,128)(2,1)}, bf16[128,512]{1,0:T(8,128)(2,1)}, bf16[128,512]{1,0:T(8,128)(2,1)}) custom-call(bf16[1024,128]{1,0:T(8,128)(2,1)S(1)} %bitcast.6, bf16[128,512]{1,0:T(8,128)(2,1)S(1)} %copy-done.1, bf16[128,512]{1,0:T(8,128)(2,1)S(1)} %copy-done.3, bf16[128,512]{1,0:T(8,128)(2,1)S(1)} %copy-done.5, ...), custom_call_target="tpu_custom_call" | custom-call | bytes 1310720 | tf_op jit(solution)/shard_map/pallas_call | solution.py:236
Async XLA Ops:
  0.6 0.9 %copy-start = (bf16[128,512]{1,0:T(8,128)(2,1)S(1)}, bf16[128,512]{1,0:T(8,128)(2,1)}, u32[]{:S(2)}) copy-start(bf16[128,512]{1,0:T(8,128)(2,1)} %outer_ref.3) | copy-start | bytes 393220
  1.5 0.9 %copy-start.2 = (bf16[128,512]{1,0:T(8,128)(2,1)S(1)}, bf16[128,512]{1,0:T(8,128)(2,1)}, u32[]{:S(2)}) copy-start(bf16[128,512]{1,0:T(8,128)(2,1)} %inner_ref.3) | copy-start | bytes 393220
  2.4 0.9 %copy-start.4 = (bf16[128,512]{1,0:T(8,128)(2,1)S(1)}, bf16[128,512]{1,0:T(8,128)(2,1)}, u32[]{:S(2)}) copy-start(bf16[128,512]{1,0:T(8,128)(2,1)} %signal_ref.3) | copy-start | bytes 393220
  3.3 0.9 %copy-start.6 = (bf16[128,512]{1,0:T(8,128)(2,1)S(1)}, bf16[128,512]{1,0:T(8,128)(2,1)}, u32[]{:S(2)}) copy-start(bf16[128,512]{1,0:T(8,128)(2,1)} %cotan_ref.3) | copy-start | bytes 393220
  4.3 19.5 %copy-start.9 = (bf16[768,256]{1,0:T(8,128)(2,1)S(1)}, bf16[768,256]{1,0:T(8,128)(2,1)}, u32[]{:S(2)}) copy-start(bf16[768,256]{1,0:T(8,128)(2,1)} %constant.12.clone.second_ref) | copy-start | bytes 1179652
  5.2 18.6 %copy-start.8 = (f32[4,16384]{1,0:T(4,128)S(1)}, f32[4,16384]{1,0:T(4,128)}, u32[]{:S(2)}) copy-start(f32[4,16384]{1,0:T(4,128)} %filt_ref.1) | copy-start | bytes 786436
  5.2 18.6 %copy-start.12 = (f32[128,256]{1,0:T(8,128)S(1)}, f32[128,256]{1,0:T(8,128)}, u32[]{:S(2)}) copy-start(f32[128,256]{1,0:T(8,128)} %constant.11.clone.twid_ref) | copy-start | bytes 393220
  5.2 18.6 %copy-start.13 = (bf16[256,256]{1,0:T(8,128)(2,1)S(1)}, bf16[256,256]{1,0:T(8,128)(2,1)}, u32[]{:S(2)}) copy-start(bf16[256,256]{1,0:T(8,128)(2,1)} %constant.10.clone.first_ref) | copy-start | bytes 393220
  5.2 34.0 %all-to-all-start = ((bf16[128,8,128]{2,1,0:T(8,128)(2,1)}), bf16[128,8,128]{2,1,0:T(8,128)(2,1)S(1)}, u32[]{:S(2)}, u32[]{:S(2)}) async-start(bf16[128,8,128]{2,1,0:T(8,128)(2,1)} %bitcast), calls=%async_computation | async-start | bytes 524288 | tf_op jit(solution)/shard_map/all_to_all | solution.py:208
  23.8 15.4 %copy-start.10 = (bf16[768,256]{1,0:T(8,128)(2,1)S(1)}, bf16[768,256]{1,0:T(8,128)(2,1)}, u32[]{:S(2)}) copy-start(bf16[768,256]{1,0:T(8,128)(2,1)} %constant.13.clone.inverse_ref) | copy-start | bytes 1179652
  23.8 15.3 %copy-start.11 = (bf16[128,768]{1,0:T(8,128)(2,1)S(1)}, bf16[128,768]{1,0:T(8,128)(2,1)}, u32[]{:S(2)}) copy-start(bf16[128,768]{1,0:T(8,128)(2,1)} %constant.14.clone.last_ref) | copy-start | bytes 589828
  42.4 20.4 %all-to-all-start.1 = ((bf16[128,8,128]{2,1,0:T(8,128)(2,1)}), bf16[128,8,128]{2,1,0:T(8,128)(2,1)S(1)}, u32[]{:S(2)}, u32[]{:S(2)}) async-start(bf16[128,8,128]{2,1,0:T(8,128)(2,1)} %bitcast.2), calls=%async_computation.1 | async-start | bytes 524288 | tf_op jit(solution)/shard_map/all_to_all | solution.py:229
  57.6 5.3 %copy-start.1 = (bf16[128,512]{1,0:T(8,128)(2,1)S(1)}, bf16[128,512]{1,0:T(8,128)(2,1)}, u32[]{:S(2)}) copy-start(bf16[128,512]{1,0:T(8,128)(2,1)} %outer_ref.3) | copy-start | bytes 393220
  57.6 5.3 %copy-start.3 = (bf16[128,512]{1,0:T(8,128)(2,1)S(1)}, bf16[128,512]{1,0:T(8,128)(2,1)}, u32[]{:S(2)}) copy-start(bf16[128,512]{1,0:T(8,128)(2,1)} %inner_ref.3) | copy-start | bytes 393220
  57.6 5.3 %copy-start.5 = (bf16[128,512]{1,0:T(8,128)(2,1)S(1)}, bf16[128,512]{1,0:T(8,128)(2,1)}, u32[]{:S(2)}) copy-start(bf16[128,512]{1,0:T(8,128)(2,1)} %signal_ref.3) | copy-start | bytes 393220
  57.6 5.3 %copy-start.7 = (bf16[128,512]{1,0:T(8,128)(2,1)S(1)}, bf16[128,512]{1,0:T(8,128)(2,1)}, u32[]{:S(2)}) copy-start(bf16[128,512]{1,0:T(8,128)(2,1)} %cotan_ref.3) | copy-start | bytes 393220

commit v2 on v1

--- a/solution.py
+++ b/solution.py
@@ -1,3 +1,4 @@
+import functools
 import math
 
 import jax
@@ -12,6 +13,19 @@
 BF = jnp.bfloat16
 F32 = jnp.float32
 VMEM_BYTES = 40 * 1024 * 1024
+VMEM_MOST = 60 * 1024 * 1024
+
+
+def member_order(count):
+    flip = count // 2
+    return [r ^ flip for r in range(count)], flip
+
+
+def flipped_copy(store, load, count, flip, height):
+    run = flip & -flip if flip else count
+    for start in range(0, count, run):
+        source = start ^ flip
+        store(slice(start * height, (start + run) * height), load(slice(source * height, (source + run) * height)))
 
 
 def split_np(table):
@@ -20,11 +34,11 @@
     return high, low
 
 
-def dft_tables(rows_n, cols_n, scale):
+def dft_tables(rows_n, cols_n, scale, order):
     length = rows_n * cols_n
     row_i = np.arange(rows_n, dtype=np.float64)
     col_i = np.arange(cols_n, dtype=np.float64)
-    ang_one = -2.0 * np.pi * np.outer(row_i + 0.25, row_i) / rows_n
+    ang_one = -2.0 * np.pi * np.outer(row_i + 0.25, row_i[order]) / rows_n
     ang_twid = -2.0 * np.pi * np.outer(row_i + 0.25, col_i) / length
     ang_two = 2.0 * np.pi * (np.outer(col_i, col_i) % cols_n) / cols_n
     first = np.concatenate([np.cos(ang_one), np.sin(ang_one)], axis=0)
@@ -55,17 +69,30 @@
     return lax.dot_general(left, right, (((1,), (0,)), ((), ())), preferred_element_type=F32)
 
 
-def pack_kernel(outer_ref, inner_ref, signal_ref, cotan_ref, out_ref, flat_ref, mix_ref):
-    prod = (inner_ref[...].astype(F32) * signal_ref[...].astype(F32)).astype(BF).astype(F32)
-    grad = (cotan_ref[...].astype(F32) * outer_ref[...].astype(F32)).astype(BF).astype(F32)
+def pack_kernel(
+    flip, outer_ref, inner_ref, signal_ref, cotan_ref, out_ref, held_ref, flat_ref, mix_ref, sems
+):
     count = out_ref.shape[0] // 8
-    for half, value in enumerate((prod, grad)):
-        flat_ref[half] = value.T
+    sources = (inner_ref, signal_ref, cotan_ref, outer_ref)
+    copies = [
+        pltpu.make_async_copy(ref, held_ref.at[k], sems.at[k]) for k, ref in enumerate(sources)
+    ]
+    for copy in copies:
+        copy.start()
+    for half in range(2):
+        copies[2 * half].wait()
+        copies[2 * half + 1].wait()
+        left, right = held_ref[2 * half].astype(F32), held_ref[2 * half + 1].astype(F32)
+        flat_ref[half] = (left * right).astype(BF).astype(F32).T
         for c in range(4):
             mix_ref[pl.ds(4 * half + c, count, stride=8), :] = flat_ref[
                 half, pl.ds(c, count, stride=4), :
             ]
-    out_ref[...] = mix_ref[...].astype(BF)
+
+    def store(rows, value):
+        out_ref[rows, :] = value
+
+    flipped_copy(store, lambda rows: mix_ref[rows, :].astype(BF), count, flip, 8)
 
 
 def second_stage(part, twid_cos, twid_sin, second):
@@ -81,11 +108,11 @@
     return dot32(jnp.concatenate(pieces, axis=0), second)
 
 
-def filter_kernel(filt_ref, first_ref, twid_ref, second_ref, out_ref, rows_ref):
+def filter_kernel(flip, filt_ref, first_ref, twid_ref, second_ref, out_ref, rows_ref):
     rows = twid_ref.shape[0]
     cols = twid_ref.shape[1] // 2
     for n in range(rows):
-        rows_ref[pl.ds(4 * n, 4), :] = filt_ref[:, cols * n : cols * (n + 1)]
+        rows_ref[pl.ds(4 * (n ^ flip), 4), :] = filt_ref[:, cols * n : cols * (n + 1)]
     first = first_ref[...]
     parts = []
     for f in range(4):
@@ -155,11 +182,21 @@
 
 
 def gate_kernel(
-    recv_ref, outer_ref, inner_ref, signal_ref, cotan_ref,
-    mixed_ref, gouter_ref, ginner_ref, gsignal_ref, flat_ref, mix_ref,
+    flip, recv_ref, outer_ref, inner_ref, signal_ref, cotan_ref, part_ref,
+    mixed_ref, gouter_ref, ginner_ref, gsignal_ref, gfilter_ref, flat_ref, mix_ref,
 ):
+    total = part_ref[0].astype(F32)
+    for g in range(1, part_ref.shape[0]):
+        total = total + part_ref[g].astype(F32)
     count = recv_ref.shape[0] // 8
-    flat_ref[...] = recv_ref[...].astype(F32)
+    cols = recv_ref.shape[1]
+    for n in range(count):
+        gfilter_ref[:, cols * (n ^ flip) : cols * ((n ^ flip) + 1)] = total[4 * n : 4 * n + 4, :]
+
+    def store(rows, value):
+        flat_ref[rows, :] = value
+
+    flipped_copy(store, lambda rows: recv_ref[rows, :].astype(F32), count, flip, 8)
     for c in range(8):
         mix_ref[c // 4, pl.ds(c % 4, count, stride=4), :] = flat_ref[pl.ds(c, count, stride=8), :]
     conv = mix_ref[0].T
@@ -170,23 +207,19 @@
     gsignal_ref[...] = (prod * inner_ref[...].astype(F32)).astype(BF)
 
 
-def sum_kernel(part_ref, out_ref):
-    rows = part_ref.shape[1] // 4
-    total = part_ref[0].astype(F32)
-    for g in range(1, part_ref.shape[0]):
-        total = total + part_ref[g].astype(F32)
-    for n in range(rows):
-        out_ref[:, 128 * n : 128 * (n + 1)] = total[4 * n : 4 * n + 4, :]
-
-
-def call(kernel, out_shape, scratch, flops=0, nbytes=0):
+def call(kernel, out_shape, scratch, flops=0, nbytes=0, vmem=VMEM_BYTES, **specs):
     return pl.pallas_call(
         kernel,
         out_shape=out_shape,
         scratch_shapes=scratch,
-        compiler_params=pltpu.CompilerParams(vmem_limit_bytes=VMEM_BYTES),
+        compiler_params=pltpu.CompilerParams(vmem_limit_bytes=vmem),
+        **specs,
         cost_estimate=pl.CostEstimate(flops=flops, bytes_accessed=nbytes, transcendentals=0),
     )
+
+
+def exchange(chunks, order):
+    return lax.all_to_all(chunks, "seq", 0, 0, axis_index_groups=[order], tiled=True)
 
 
 def body(gate_outer, gate_inner, signal, filter_raw, cotangent):
@@ -194,20 +227,28 @@
     seq_parts = lax.axis_size("seq")
     rows, cols = seq_parts, tok_rows
     seq_len = rows * cols
-    tables = dft_tables(rows, cols, 1.0 / math.sqrt(seq_len) / seq_len)
+    order, flip = member_order(seq_parts)
+    tables = dft_tables(rows, cols, 1.0 / math.sqrt(seq_len) / seq_len, order)
     first, twid = jnp.asarray(tables["first"]), jnp.asarray(tables["twid"])
     second, inverse = jnp.asarray(tables["second"]), jnp.asarray(tables["inverse"])
     last = jnp.asarray(tables["last"])
     wide = 8 * rows
     packed = call(
-        pack_kernel,
+        functools.partial(pack_kernel, flip),
         jax.ShapeDtypeStruct((wide, cols), BF),
-        [pltpu.VMEM((2, chan_cols, tok_rows), F32), pltpu.VMEM((wide, cols), F32)],
+        [
+            pltpu.VMEM((4, tok_rows, chan_cols), BF),
+            pltpu.VMEM((2, chan_cols, tok_rows), F32),
+            pltpu.VMEM((wide, cols), F32),
+            pltpu.SemaphoreType.DMA((4,)),
+        ],
         nbytes=6 * 2 * tok_rows * chan_cols,
+        vmem=VMEM_MOST,
+        in_specs=[pl.BlockSpec(memory_space=pltpu.HBM)] * 4,
     )(gate_outer, gate_inner, signal, cotangent)
-    received = lax.all_to_all(packed.reshape(rows, 8, cols), "seq", 0, 0, tiled=True)
+    received = exchange(packed.reshape(rows, 8, cols), order)
     tap_spec = call(
-        filter_kernel,
+        functools.partial(filter_kernel, flip),
         jax.ShapeDtypeStruct((4 * rows, 2 * cols), F32),
         [pltpu.VMEM((4 * rows, cols), F32)],
         flops=10**9, nbytes=10**6,
@@ -226,20 +267,14 @@
         flops=3 * 10**9, nbytes=2 * 10**6,
     )(received.reshape(wide, cols), tap_spec, first, twid, second, inverse, last)
     parts = lax.all_gather(corr, "chan", axis=0, tiled=False)
-    returned = lax.all_to_all(send.reshape(rows, 8, cols), "seq", 0, 0, tiled=True)
-    grad_filter = call(
-        sum_kernel,
-        jax.ShapeDtypeStruct(filter_raw.shape, F32),
-        [],
-        nbytes=10**6,
-    )(parts)
-    outs = call(
-        gate_kernel,
-        tuple(jax.ShapeDtypeStruct((tok_rows, chan_cols), BF) for _ in range(4)),
+    returned = exchange(send.reshape(rows, 8, cols), order)
+    block = jax.ShapeDtypeStruct((tok_rows, chan_cols), BF)
+    return call(
+        functools.partial(gate_kernel, flip),
+        (block, block, block, block, jax.ShapeDtypeStruct(filter_raw.shape, F32)),
         [pltpu.VMEM((wide, cols), F32), pltpu.VMEM((2, chan_cols, tok_rows), F32)],
-        nbytes=10 * 2 * tok_rows * chan_cols,
-    )(returned.reshape(wide, cols), gate_outer, gate_inner, signal, cotangent)
-    return (*outs, grad_filter)
+        nbytes=12 * 2 * tok_rows * chan_cols,
+    )(returned.reshape(wide, cols), gate_outer, gate_inner, signal, cotangent, parts)
 
 
 def solution(mesh):

time: 64.2 us -> 59.9 us (0.933)
  the two profiles are of different devices: /device:TPU:4 before, /device:TPU:1 now
where the time goes in v2:
time: 59.9 us; the launch traced here: 59.6 us
  starting transfers between devices  29.7 us (50%)
  blocking collectives  12.5 us (21%)
  waiting for transfers between devices  9.42 us (16%)
  Pallas kernels  7.12 us (12%)
  between operations  0.79 us (1%)
    all_to_all x2, starting transfers between devices, exchange(): lax.all_to_all(chunks, 'seq', 0, 0, axis_index_groups=[order], tiled=True)  29.7 us
    all_gather x1, blocking collectives, body(): parts = lax.all_gather(corr, 'chan', axis=0, tiled=False)  12.5 us
    all_to_all x2, waiting for transfers between devices, exchange(): lax.all_to_all(chunks, 'seq', 0, 0, axis_index_groups=[order], tiled=True)  9.42 us
    pallas_call x1, Pallas kernels, body(): call(conv_kernel, (jax.ShapeDtypeStruct((wide, cols), BF), jax.ShapeDtype...  3.27 us
    pallas_call x1, Pallas kernels, body(): call(functools.partial(pack_kernel, flip), jax.ShapeDtypeStruct((wide, co...  2.08 us
  transfers between devices with their start and end apart: 2, of which 1 were waited for; matrix products, arithmetic and copies ran while one was open for 0% of the time, Pallas kernels for 1%

profile of v2, /device:TPU:1, one launch (start us, length us, event | category | flops | bytes accessed | tf_op | source)
XLA Modules:
  0.0 59.6 jit_solution(6377060876016953432)
XLA Ops:
  0.6 0.0 copy-start.5
  0.6 2.1 %shard_map.137 = bf16[1024,128]{1,0:T(8,128)(2,1)} custom-call(bf16[128,512]{1,0:T(8,128)(2,1)} %outer_ref.3, bf16[128,512]{1,0:T(8,128)(2,1)} %inner_ref.3, bf16[128,512]{1,0:T(8,128)(2,1)} %signal_ref.3, bf16[128,512]{1,0:T(8,128)(2,1)} %cotan_ref.3), custom_call_target="tpu_custom_call" | custom-call | bytes 786432 | tf_op jit(solution)/shard_map/pallas_call | solution.py:236
  2.7 0.0 copy-start.4
  2.7 0.0 copy-start.8
  2.8 0.0 copy-start.9
  2.8 19.5 %all-to-all-start = ((bf16[128,8,128]{2,1,0:T(8,128)(2,1)}), bf16[128,8,128]{2,1,0:T(8,128)(2,1)S(1)}, u32[]{:S(2)}, u32[]{:S(2)}) async-start(bf16[128,8,128]{2,1,0:T(8,128)(2,1)} %bitcast.8), calls=%async_computation | async-start | bytes 524288 | tf_op jit(solution)/shard_map/all_to_all | solution.py:222
  22.3 0.0 copy-done.5
  22.3 0.0 copy-done.4
  22.3 0.0 copy-done.8
  22.3 0.0 copy-done.9
  22.3 0.0 copy-start.6
  22.3 0.0 copy-start.7
  22.3 0.7 %shard_map.138.spec_ref = f32[512,256]{1,0:T(8,128)S(1)} custom-call(f32[4,16384]{1,0:T(4,128)S(1)} %copy-done.4, bf16[256,256]{1,0:T(8,128)(2,1)S(1)} %copy-done.9, f32[128,256]{1,0:T(8,128)S(1)} %copy-done.8, bf16[768,256]{1,0:T(8,128)(2,1)S(1)} %copy-done.5), custom_call_target="tpu_custom_call" | custom-call | flops 1000000000 | bytes 1000000 | tf_op jit(solution)/shard_map/pallas_call | solution.py:250
  23.0 9.4 %all-to-all-done = bf16[128,8,128]{2,1,0:T(8,128)(2,1)S(1)} async-done(((bf16[128,8,128]{2,1,0:T(8,128)(2,1)}), bf16[128,8,128]{2,1,0:T(8,128)(2,1)S(1)}, u32[]{:S(2)}, u32[]{:S(2)}) %all-to-all-start) | async-done | bytes 262176 | tf_op jit(solution)/shard_map/all_to_all | solution.py:222
  32.4 0.0 copy-done.6
  32.4 0.0 copy-done.7
  32.4 3.3 %shard_map.139 = (bf16[1024,128]{1,0:T(8,128)(2,1)}, bf16[512,128]{1,0:T(8,128)(2,1)S(1)}) custom-call(bf16[1024,128]{1,0:T(8,128)(2,1)S(1)} %bitcast.7, f32[512,256]{1,0:T(8,128)S(1)} %shard_map.138.spec_ref, bf16[256,256]{1,0:T(8,128)(2,1)S(1)} %copy-done.9, f32[128,256]{1,0:T(8,128)S(1)} %copy-done.8, bf16[768,256]{1,0:T(8,128)(2,1)S(1)} %copy-done.5, ...), custom_call_target="tpu_custom_call" | custom-call | flops 3000000000 | bytes 2000000 | tf_op jit(solution)/shard_map/pallas_call | solution.py:256
  35.7 10.2 %all-to-all-start.1 = ((bf16[128,8,128]{2,1,0:T(8,128)(2,1)}), bf16[128,8,128]{2,1,0:T(8,128)(2,1)S(1)}, u32[]{:S(2)}, u32[]{:S(2)}) async-start(bf16[128,8,128]{2,1,0:T(8,128)(2,1)} %bitcast.2), calls=%async_computation.1 | async-start | bytes 524288 | tf_op jit(solution)/shard_map/all_to_all | solution.py:222
  45.9 0.0 copy-start
  45.9 0.0 copy-start.1
  45.9 0.0 copy-start.2
  45.9 0.0 copy-start.3
  45.9 12.5 %all-gather = bf16[2048,128]{1,0:T(8,128)(2,1)S(1)} all-gather(bf16[512,128]{1,0:T(8,128)(2,1)S(1)} %get-tuple-element.8), channel_id=2, replica_groups=mesh['seq'=128,'chan'=4] {'chan'}, dimensions={0}, use_global_device_ids=true | all-gather | bytes 655360 | tf_op jit(solution)/shard_map/all_gather | solution.py:269
  58.5 0.0 all-to-all-done.1
  58.5 0.0 copy-done
  58.5 0.0 copy-done.1
  58.5 0.0 copy-done.2
  58.5 0.0 copy-done.3
  58.5 1.1 %shard_map.140 = (bf16[128,512]{1,0:T(8,128)(2,1)}, bf16[128,512]{1,0:T(8,128)(2,1)}, bf16[128,512]{1,0:T(8,128)(2,1)}, bf16[128,512]{1,0:T(8,128)(2,1)}, f32[4,16384]{1,0:T(4,128)}) custom-call(bf16[1024,128]{1,0:T(8,128)(2,1)S(1)} %bitcast.6, bf16[128,512]{1,0:T(8,128)(2,1)S(1)} %copy-done, bf16[128,512]{1,0:T(8,128)(2,1)S(1)} %copy-done.1, ...), custom_call_target="tpu_custom_call" | custom-call | bytes 1572864 | tf_op jit(solution)/shard_map/pallas_call | solution.py:272
Async XLA Ops:
  0.6 21.6 %copy-start.5 = (bf16[768,256]{1,0:T(8,128)(2,1)S(1)}, bf16[768,256]{1,0:T(8,128)(2,1)}, u32[]{:S(2)}) copy-start(bf16[768,256]{1,0:T(8,128)(2,1)} %constant.12.clone.second_ref) | copy-start | bytes 1179652
  2.7 19.5 %copy-start.4 = (f32[4,16384]{1,0:T(4,128)S(1)}, f32[4,16384]{1,0:T(4,128)}, u32[]{:S(2)}) copy-start(f32[4,16384]{1,0:T(4,128)} %filt_ref.1) | copy-start | bytes 786436
  2.7 19.5 %copy-start.8 = (f32[128,256]{1,0:T(8,128)S(1)}, f32[128,256]{1,0:T(8,128)}, u32[]{:S(2)}) copy-start(f32[128,256]{1,0:T(8,128)} %constant.11.clone.twid_ref) | copy-start | bytes 393220
  2.8 19.5 %copy-start.9 = (bf16[256,256]{1,0:T(8,128)(2,1)S(1)}, bf16[256,256]{1,0:T(8,128)(2,1)}, u32[]{:S(2)}) copy-start(bf16[256,256]{1,0:T(8,128)(2,1)} %constant.10.clone.first_ref) | copy-start | bytes 393220
  2.8 29.7 %all-to-all-start = ((bf16[128,8,128]{2,1,0:T(8,128)(2,1)}), bf16[128,8,128]{2,1,0:T(8,128)(2,1)S(1)}, u32[]{:S(2)}, u32[]{:S(2)}) async-start(bf16[128,8,128]{2,1,0:T(8,128)(2,1)} %bitcast.8), calls=%async_computation | async-start | bytes 524288 | tf_op jit(solution)/shard_map/all_to_all | solution.py:222
  22.3 10.1 %copy-start.6 = (bf16[768,256]{1,0:T(8,128)(2,1)S(1)}, bf16[768,256]{1,0:T(8,128)(2,1)}, u32[]{:S(2)}) copy-start(bf16[768,256]{1,0:T(8,128)(2,1)} %constant.13.clone.inverse_ref) | copy-start | bytes 1179652
  22.3 10.1 %copy-start.7 = (bf16[128,768]{1,0:T(8,128)(2,1)S(1)}, bf16[128,768]{1,0:T(8,128)(2,1)}, u32[]{:S(2)}) copy-start(bf16[128,768]{1,0:T(8,128)(2,1)} %constant.14.clone.last_ref) | copy-start | bytes 589828
  35.7 22.8 %all-to-all-start.1 = ((bf16[128,8,128]{2,1,0:T(8,128)(2,1)}), bf16[128,8,128]{2,1,0:T(8,128)(2,1)S(1)}, u32[]{:S(2)}, u32[]{:S(2)}) async-start(bf16[128,8,128]{2,1,0:T(8,128)(2,1)} %bitcast.2), calls=%async_computation.1 | async-start | bytes 524288 | tf_op jit(solution)/shard_map/all_to_all | solution.py:222
  45.9 12.6 %copy-start = (bf16[128,512]{1,0:T(8,128)(2,1)S(1)}, bf16[128,512]{1,0:T(8,128)(2,1)}, u32[]{:S(2)}) copy-start(bf16[128,512]{1,0:T(8,128)(2,1)} %outer_ref.3) | copy-start | bytes 393220
  45.9 12.6 %copy-start.1 = (bf16[128,512]{1,0:T(8,128)(2,1)S(1)}, bf16[128,512]{1,0:T(8,128)(2,1)}, u32[]{:S(2)}) copy-start(bf16[128,512]{1,0:T(8,128)(2,1)} %inner_ref.3) | copy-start | bytes 393220
  45.9 12.6 %copy-start.2 = (bf16[128,512]{1,0:T(8,128)(2,1)S(1)}, bf16[128,512]{1,0:T(8,128)(2,1)}, u32[]{:S(2)}) copy-start(bf16[128,512]{1,0:T(8,128)(2,1)} %signal_ref.3) | copy-start | bytes 393220
  45.9 12.6 %copy-start.3 = (bf16[128,512]{1,0:T(8,128)(2,1)S(1)}, bf16[128,512]{1,0:T(8,128)(2,1)}, u32[]{:S(2)}) copy-start(bf16[128,512]{1,0:T(8,128)(2,1)} %cotan_ref.3) | copy-start | bytes 393220

commit v3 on v2

--- a/solution.py
+++ b/solution.py
@@ -17,7 +17,7 @@
 
 
 def member_order(count):
-    flip = count // 2
+    flip = count // 2 + count // 4
     return [r ^ flip for r in range(count)], flip
 
 
@@ -54,8 +54,8 @@
         first=np.concatenate([first_h, first_l], axis=1),
         twid=np.concatenate([np.cos(ang_twid), -np.sin(ang_twid)], axis=1).astype(np.float32),
         second=np.concatenate([second_h, second_h, second_l], axis=0),
-        inverse=np.concatenate([inv_h, inv_h, inv_l], axis=0),
-        last=np.concatenate([last_h, last_l, last_h], axis=1),
+        inverse=np.concatenate([inv_h, inv_l], axis=0),
+        last=np.concatenate([last_h, last_l], axis=1),
     )
 
 
@@ -161,17 +161,16 @@
     products.sort(key=lambda item: item[0])
     pieces = []
     for _, real, imag in products:
-        high, low = split_hl(jnp.concatenate([real, imag], axis=1))
-        pieces.append(jnp.concatenate([high, low, high], axis=1))
+        value = jnp.concatenate([real, imag], axis=1).astype(BF)
+        pieces.append(jnp.concatenate([value, value], axis=1))
     turned = dot32(jnp.concatenate(pieces, axis=0), inverse_ref[...])
     columns = []
     for c in range(12):
         real, imag = parts_of(turned, c)
         value = jnp.concatenate(
             [real * twid_cos - imag * twid_sin, imag * twid_cos + real * twid_sin], axis=0
-        )
-        high, low = split_hl(value)
-        columns.append(jnp.concatenate([high, high, low], axis=0))
+        ).astype(BF)
+        columns.append(jnp.concatenate([value, value], axis=0))
     result = dot32(last_ref[...], jnp.concatenate(columns, axis=1))
     for c in range(8):
         back_ref[pl.ds(c, rows, stride=8), :] = result[:, cols * c : cols * (c + 1)]

time: 59.9 us -> 59.1 us (0.987)
  starting transfers between devices: 29.7 us -> 27.7 us
  waiting for transfers between devices: 9.42 us -> 11 us
    all_to_all x2, starting transfers between devices: 29.7 us -> 27.7 us  [exchange(): lax.all_to_all(chunks, 'seq', 0, 0, axis_index_groups=[order], tiled=True)]
    all_to_all x2, waiting for transfers between devices: 9.42 us -> 11 us  [exchange(): lax.all_to_all(chunks, 'seq', 0, 0, axis_index_groups=[order], tiled=True)]
where the time goes in v3:
time: 59.1 us; the launch traced here: 58.9 us
  starting transfers between devices  27.7 us (47%)
  blocking collectives  12.7 us (21%)
  waiting for transfers between devices  11 us (19%)
  Pallas kernels  6.6 us (11%)
  between operations  0.79 us (1%)
    all_to_all x2, starting transfers between devices, exchange(): lax.all_to_all(chunks, 'seq', 0, 0, axis_index_groups=[order], tiled=True)  27.7 us
    all_gather x1, blocking collectives, body(): parts = lax.all_gather(corr, 'chan', axis=0, tiled=False)  12.7 us
    all_to_all x2, waiting for transfers between devices, exchange(): lax.all_to_all(chunks, 'seq', 0, 0, axis_index_groups=[order], tiled=True)  11 us
    pallas_call x1, Pallas kernels, body(): call(conv_kernel, (jax.ShapeDtypeStruct((wide, cols), BF), jax.ShapeDtype...  2.74 us
    pallas_call x1, Pallas kernels, body(): call(functools.partial(pack_kernel, flip), jax.ShapeDtypeStruct((wide, co...  2.08 us
  transfers between devices with their start and end apart: 2, of which 1 were waited for; matrix products, arithmetic and copies ran while one was open for 0% of the time, Pallas kernels for 1%

profile of v3, /device:TPU:1, one launch (start us, length us, event | category | flops | bytes accessed | tf_op | source)
XLA Modules:
  0.0 58.9 jit_solution(4577944070286558602)
XLA Ops:
  0.6 0.0 copy-start.5
  0.6 2.1 %shard_map.137 = bf16[1024,128]{1,0:T(8,128)(2,1)} custom-call(bf16[128,512]{1,0:T(8,128)(2,1)} %outer_ref.3, bf16[128,512]{1,0:T(8,128)(2,1)} %inner_ref.3, bf16[128,512]{1,0:T(8,128)(2,1)} %signal_ref.3, bf16[128,512]{1,0:T(8,128)(2,1)} %cotan_ref.3), custom_call_target="tpu_custom_call" | custom-call | bytes 786432 | tf_op jit(solution)/shard_map/pallas_call | solution.py:235
  2.7 0.0 copy-start.4
  2.7 0.0 copy-start.7
  2.8 0.0 copy-start.8
  2.8 19.4 %all-to-all-start = ((bf16[128,8,128]{2,1,0:T(8,128)(2,1)}), bf16[128,8,128]{2,1,0:T(8,128)(2,1)S(1)}, u32[]{:S(2)}, u32[]{:S(2)}) async-start(bf16[128,8,128]{2,1,0:T(8,128)(2,1)} %bitcast.8), calls=%async_computation | async-start | bytes 524288 | tf_op jit(solution)/shard_map/all_to_all | solution.py:221
  22.1 0.0 copy-done.5
  22.1 0.0 copy-done.4
  22.2 0.0 copy-done.7
  22.2 0.0 copy-done.8
  22.2 0.0 copy-start.6
  22.2 0.0 copy-start.9
  22.2 0.7 %shard_map.138.spec_ref = f32[512,256]{1,0:T(8,128)S(1)} custom-call(f32[4,16384]{1,0:T(4,128)S(1)} %copy-done.4, bf16[256,256]{1,0:T(8,128)(2,1)S(1)} %copy-done.8, f32[128,256]{1,0:T(8,128)S(1)} %copy-done.7, bf16[768,256]{1,0:T(8,128)(2,1)S(1)} %copy-done.5), custom_call_target="tpu_custom_call" | custom-call | flops 1000000000 | bytes 1000000 | tf_op jit(solution)/shard_map/pallas_call | solution.py:249
  22.9 11.0 %all-to-all-done = bf16[128,8,128]{2,1,0:T(8,128)(2,1)S(1)} async-done(((bf16[128,8,128]{2,1,0:T(8,128)(2,1)}), bf16[128,8,128]{2,1,0:T(8,128)(2,1)S(1)}, u32[]{:S(2)}, u32[]{:S(2)}) %all-to-all-start) | async-done | bytes 262176 | tf_op jit(solution)/shard_map/all_to_all | solution.py:221
  33.9 0.0 copy-done.6
  33.9 0.0 copy-done.9
  33.9 2.7 %shard_map.139 = (bf16[1024,128]{1,0:T(8,128)(2,1)}, bf16[512,128]{1,0:T(8,128)(2,1)S(1)}) custom-call(bf16[1024,128]{1,0:T(8,128)(2,1)S(1)} %bitcast.7, f32[512,256]{1,0:T(8,128)S(1)} %shard_map.138.spec_ref, bf16[256,256]{1,0:T(8,128)(2,1)S(1)} %copy-done.8, f32[128,256]{1,0:T(8,128)S(1)} %copy-done.7, bf16[768,256]{1,0:T(8,128)(2,1)S(1)} %copy-done.5, ...), custom_call_target="tpu_custom_call" | custom-call | flops 3000000000 | bytes 2000000 | tf_op jit(solution)/shard_map/pallas_call | solution.py:255
  36.6 8.3 %all-to-all-start.1 = ((bf16[128,8,128]{2,1,0:T(8,128)(2,1)}), bf16[128,8,128]{2,1,0:T(8,128)(2,1)S(1)}, u32[]{:S(2)}, u32[]{:S(2)}) async-start(bf16[128,8,128]{2,1,0:T(8,128)(2,1)} %bitcast.2), calls=%async_computation.1 | async-start | bytes 524288 | tf_op jit(solution)/shard_map/all_to_all | solution.py:221
  45.0 0.0 copy-start
  45.0 0.0 copy-start.1
  45.0 0.0 copy-start.2
  45.0 0.0 copy-start.3
  45.0 12.7 %all-gather = bf16[2048,128]{1,0:T(8,128)(2,1)S(1)} all-gather(bf16[512,128]{1,0:T(8,128)(2,1)S(1)} %get-tuple-element.8), channel_id=2, replica_groups=mesh['seq'=128,'chan'=4] {'chan'}, dimensions={0}, use_global_device_ids=true | all-gather | bytes 655360 | tf_op jit(solution)/shard_map/all_gather | solution.py:268
  57.7 0.0 all-to-all-done.1
  57.7 0.0 copy-done
  57.8 0.0 copy-done.1
  57.8 0.0 copy-done.2
  57.8 0.0 copy-done.3
  57.8 1.1 %shard_map.140 = (bf16[128,512]{1,0:T(8,128)(2,1)}, bf16[128,512]{1,0:T(8,128)(2,1)}, bf16[128,512]{1,0:T(8,128)(2,1)}, bf16[128,512]{1,0:T(8,128)(2,1)}, f32[4,16384]{1,0:T(4,128)}) custom-call(bf16[1024,128]{1,0:T(8,128)(2,1)S(1)} %bitcast.6, bf16[128,512]{1,0:T(8,128)(2,1)S(1)} %copy-done, bf16[128,512]{1,0:T(8,128)(2,1)S(1)} %copy-done.1, ...), custom_call_target="tpu_custom_call" | custom-call | bytes 1572864 | tf_op jit(solution)/shard_map/pallas_call | solution.py:271
Async XLA Ops:
  0.6 21.5 %copy-start.5 = (bf16[768,256]{1,0:T(8,128)(2,1)S(1)}, bf16[768,256]{1,0:T(8,128)(2,1)}, u32[]{:S(2)}) copy-start(bf16[768,256]{1,0:T(8,128)(2,1)} %constant.12.clone.second_ref) | copy-start | bytes 1179652
  2.7 19.4 %copy-start.4 = (f32[4,16384]{1,0:T(4,128)S(1)}, f32[4,16384]{1,0:T(4,128)}, u32[]{:S(2)}) copy-start(f32[4,16384]{1,0:T(4,128)} %filt_ref.1) | copy-start | bytes 786436
  2.7 19.4 %copy-start.7 = (f32[128,256]{1,0:T(8,128)S(1)}, f32[128,256]{1,0:T(8,128)}, u32[]{:S(2)}) copy-start(f32[128,256]{1,0:T(8,128)} %constant.11.clone.twid_ref) | copy-start | bytes 393220
  2.8 19.4 %copy-start.8 = (bf16[256,256]{1,0:T(8,128)(2,1)S(1)}, bf16[256,256]{1,0:T(8,128)(2,1)}, u32[]{:S(2)}) copy-start(bf16[256,256]{1,0:T(8,128)(2,1)} %constant.10.clone.first_ref) | copy-start | bytes 393220
  2.8 31.1 %all-to-all-start = ((bf16[128,8,128]{2,1,0:T(8,128)(2,1)}), bf16[128,8,128]{2,1,0:T(8,128)(2,1)S(1)}, u32[]{:S(2)}, u32[]{:S(2)}) async-start(bf16[128,8,128]{2,1,0:T(8,128)(2,1)} %bitcast.8), calls=%async_computation | async-start | bytes 524288 | tf_op jit(solution)/shard_map/all_to_all | solution.py:221
  22.2 11.7 %copy-start.6 = (bf16[512,256]{1,0:T(8,128)(2,1)S(1)}, bf16[512,256]{1,0:T(8,128)(2,1)}, u32[]{:S(2)}) copy-start(bf16[512,256]{1,0:T(8,128)(2,1)} %constant.13.clone.inverse_ref) | copy-start | bytes 786436
  22.2 11.7 %copy-start.9 = (bf16[128,512]{1,0:T(8,128)(2,1)S(1)}, bf16[128,512]{1,0:T(8,128)(2,1)}, u32[]{:S(2)}) copy-start(bf16[128,512]{1,0:T(8,128)(2,1)} %constant.14.clone.last_ref) | copy-start | bytes 393220
  36.6 21.1 %all-to-all-start.1 = ((bf16[128,8,128]{2,1,0:T(8,128)(2,1)}), bf16[128,8,128]{2,1,0:T(8,128)(2,1)S(1)}, u32[]{:S(2)}, u32[]{:S(2)}) async-start(bf16[128,8,128]{2,1,0:T(8,128)(2,1)} %bitcast.2), calls=%async_computation.1 | async-start | bytes 524288 | tf_op jit(solution)/shard_map/all_to_all | solution.py:221
  45.0 12.8 %copy-start = (bf16[128,512]{1,0:T(8,128)(2,1)S(1)}, bf16[128,512]{1,0:T(8,128)(2,1)}, u32[]{:S(2)}) copy-start(bf16[128,512]{1,0:T(8,128)(2,1)} %outer_ref.3) | copy-start | bytes 393220
  45.0 12.7 %copy-start.1 = (bf16[128,512]{1,0:T(8,128)(2,1)S(1)}, bf16[128,512]{1,0:T(8,128)(2,1)}, u32[]{:S(2)}) copy-start(bf16[128,512]{1,0:T(8,128)(2,1)} %inner_ref.3) | copy-start | bytes 393220
  45.0 12.7 %copy-start.2 = (bf16[128,512]{1,0:T(8,128)(2,1)S(1)}, bf16[128,512]{1,0:T(8,128)(2,1)}, u32[]{:S(2)}) copy-start(bf16[128,512]{1,0:T(8,128)(2,1)} %signal_ref.3) | copy-start | bytes 393220
  45.0 12.7 %copy-start.3 = (bf16[128,512]{1,0:T(8,128)(2,1)S(1)}, bf16[128,512]{1,0:T(8,128)(2,1)}, u32[]{:S(2)}) copy-start(bf16[128,512]{1,0:T(8,128)(2,1)} %cotan_ref.3) | copy-start | bytes 393220

commit v4 on v3

--- a/solution.py
+++ b/solution.py
@@ -131,7 +131,7 @@
 
 def conv_kernel(
     recv_ref, spec_ref, first_ref, twid_ref, second_ref, inverse_ref, last_ref,
-    send_ref, corr_ref, flat_ref, back_ref, corr_mix_ref,
+    send_ref, corr_ref, flat_ref, back_ref, corr_mix_ref, done_ref, sem,
 ):
     rows = twid_ref.shape[0]
     cols = twid_ref.shape[1] // 2
@@ -150,34 +150,40 @@
         block = array[rows * c : rows * (c + 1)]
         return block[:, :cols], block[:, cols:]
 
-    products = []
+    def inverse_of(products):
+        pieces = []
+        for real, imag in products:
+            value = jnp.concatenate([real, imag], axis=1).astype(BF)
+            pieces.append(jnp.concatenate([value, value], axis=1))
+        turned = dot32(jnp.concatenate(pieces, axis=0), inverse_ref[...])
+        columns = []
+        for c in range(len(products)):
+            real, imag = parts_of(turned, c)
+            value = jnp.concatenate(
+                [real * twid_cos - imag * twid_sin, imag * twid_cos + real * twid_sin], axis=0
+            ).astype(BF)
+            columns.append(jnp.concatenate([value, value], axis=0))
+        return dot32(last_ref[...], jnp.concatenate(columns, axis=1))
+
+    convs, backs, corrs = [], [], []
     for c in range(4):
-        tap_r, tap_i = spec_ref[rows * c : rows * (c + 1), :cols], spec_ref[rows * c : rows * (c + 1), cols:]
+        tap_r, tap_i = parts_of(spec_ref, c)
         in_r, in_i = parts_of(spec, c)
         gr_r, gr_i = parts_of(spec, 4 + c)
-        products.append((4 * 0 + c, tap_r * in_r - tap_i * in_i, tap_r * in_i + tap_i * in_r))
-        products.append((4 * 1 + c, tap_r * gr_r + tap_i * gr_i, tap_r * gr_i - tap_i * gr_r))
-        products.append((4 * 2 + c, in_r * gr_r + in_i * gr_i, in_r * gr_i - in_i * gr_r))
-    products.sort(key=lambda item: item[0])
-    pieces = []
-    for _, real, imag in products:
-        value = jnp.concatenate([real, imag], axis=1).astype(BF)
-        pieces.append(jnp.concatenate([value, value], axis=1))
-    turned = dot32(jnp.concatenate(pieces, axis=0), inverse_ref[...])
-    columns = []
-    for c in range(12):
-        real, imag = parts_of(turned, c)
-        value = jnp.concatenate(
-            [real * twid_cos - imag * twid_sin, imag * twid_cos + real * twid_sin], axis=0
-        ).astype(BF)
-        columns.append(jnp.concatenate([value, value], axis=0))
-    result = dot32(last_ref[...], jnp.concatenate(columns, axis=1))
+        convs.append((tap_r * in_r - tap_i * in_i, tap_r * in_i + tap_i * in_r))
+        backs.append((tap_r * gr_r + tap_i * gr_i, tap_r * gr_i - tap_i * gr_r))
+        corrs.append((in_r * gr_r + in_i * gr_i, in_r * gr_i - in_i * gr_r))
+    result = inverse_of(convs + backs)
     for c in range(8):
         back_ref[pl.ds(c, rows, stride=8), :] = result[:, cols * c : cols * (c + 1)]
-    send_ref[...] = back_ref[...].astype(BF)
+    done_ref[...] = back_ref[...].astype(BF)
+    copy = pltpu.make_async_copy(done_ref, send_ref, sem)
+    copy.start()
+    result = inverse_of(corrs)
     for c in range(4):
-        corr_mix_ref[pl.ds(c, rows, stride=4), :] = result[:, cols * (8 + c) : cols * (9 + c)]
-    corr_ref[...] = corr_mix_ref[...].astype(corr_ref.dtype)
+        corr_mix_ref[pl.ds(c, rows, stride=4), :] = result[:, cols * c : cols * (c + 1)]
+    corr_ref[...] = corr_mix_ref[...].astype(BF)
+    copy.wait()
 
 
 def gate_kernel(
@@ -262,8 +268,14 @@
             pltpu.VMEM((wide, cols), F32),
             pltpu.VMEM((wide, cols), F32),
             pltpu.VMEM((4 * rows, cols), F32),
+            pltpu.VMEM((wide, cols), BF),
+            pltpu.SemaphoreType.DMA,
         ],
         flops=3 * 10**9, nbytes=2 * 10**6,
+        out_specs=(
+            pl.BlockSpec(memory_space=pltpu.HBM),
+            pl.BlockSpec(memory_space=pltpu.VMEM),
+        ),
     )(received.reshape(wide, cols), tap_spec, first, twid, second, inverse, last)
     parts = lax.all_gather(corr, "chan", axis=0, tiled=False)
     returned = exchange(send.reshape(rows, 8, cols), order)

time: 59.1 us -> 59 us (level)
  no operation moved by 1% of the time
where the time goes in v4:
time: 59 us; the launch traced here: 58.7 us
  starting transfers between devices  27.7 us (47%)
  blocking collectives  12.7 us (22%)
  waiting for transfers between devices  11 us (19%)
  Pallas kernels  6.45 us (11%)
  between operations  0.8 us (1%)
    all_to_all x2, starting transfers between devices, exchange(): lax.all_to_all(chunks, 'seq', 0, 0, axis_index_groups=[order], tiled=True)  27.7 us
    all_gather x1, blocking collectives, body(): parts = lax.all_gather(corr, 'chan', axis=0, tiled=False)  12.7 us
    all_to_all x2, waiting for transfers between devices, exchange(): lax.all_to_all(chunks, 'seq', 0, 0, axis_index_groups=[order], tiled=True)  11 us
    pallas_call x1, Pallas kernels, body(): call(conv_kernel, (jax.ShapeDtypeStruct((wide, cols), BF), jax.ShapeDtype...  2.59 us
    pallas_call x1, Pallas kernels, body(): call(functools.partial(pack_kernel, flip), jax.ShapeDtypeStruct((wide, co...  2.08 us
  transfers between devices with their start and end apart: 2, of which 1 were waited for; matrix products, arithmetic and copies ran while one was open for 0% of the time, Pallas kernels for 1%

profile of v4, /device:TPU:1, one launch (start us, length us, event | category | flops | bytes accessed | tf_op | source)
XLA Modules:
  0.0 58.7 jit_solution(1017502131321323988)
XLA Ops:
  0.6 0.0 copy-start.5
  0.6 2.1 %shard_map.137 = bf16[1024,128]{1,0:T(8,128)(2,1)} custom-call(bf16[128,512]{1,0:T(8,128)(2,1)} %outer_ref.3, bf16[128,512]{1,0:T(8,128)(2,1)} %inner_ref.3, bf16[128,512]{1,0:T(8,128)(2,1)} %signal_ref.3, bf16[128,512]{1,0:T(8,128)(2,1)} %cotan_ref.3), custom_call_target="tpu_custom_call" | custom-call | bytes 786432 | tf_op jit(solution)/shard_map/pallas_call | solution.py:241
  2.7 0.0 copy-start.4
  2.7 0.0 copy-start.7
  2.8 0.0 copy-start.8
  2.8 19.4 %all-to-all-start = ((bf16[128,8,128]{2,1,0:T(8,128)(2,1)}), bf16[128,8,128]{2,1,0:T(8,128)(2,1)S(1)}, u32[]{:S(2)}, u32[]{:S(2)}) async-start(bf16[128,8,128]{2,1,0:T(8,128)(2,1)} %bitcast.8), calls=%async_computation | async-start | bytes 524288 | tf_op jit(solution)/shard_map/all_to_all | solution.py:227
  22.1 0.0 copy-done.5
  22.1 0.0 copy-done.4
  22.2 0.0 copy-done.7
  22.2 0.0 copy-done.8
  22.2 0.0 copy-start.6
  22.2 0.0 copy-start.9
  22.2 0.7 %shard_map.138.spec_ref = f32[512,256]{1,0:T(8,128)S(1)} custom-call(f32[4,16384]{1,0:T(4,128)S(1)} %copy-done.4, bf16[256,256]{1,0:T(8,128)(2,1)S(1)} %copy-done.8, f32[128,256]{1,0:T(8,128)S(1)} %copy-done.7, bf16[768,256]{1,0:T(8,128)(2,1)S(1)} %copy-done.5), custom_call_target="tpu_custom_call" | custom-call | flops 1000000000 | bytes 1000000 | tf_op jit(solution)/shard_map/pallas_call | solution.py:255
  22.9 11.0 %all-to-all-done = bf16[128,8,128]{2,1,0:T(8,128)(2,1)S(1)} async-done(((bf16[128,8,128]{2,1,0:T(8,128)(2,1)}), bf16[128,8,128]{2,1,0:T(8,128)(2,1)S(1)}, u32[]{:S(2)}, u32[]{:S(2)}) %all-to-all-start) | async-done | bytes 262176 | tf_op jit(solution)/shard_map/all_to_all | solution.py:227
  33.9 0.0 copy-done.6
  33.9 0.0 copy-done.9
  33.9 2.6 %shard_map.139 = (bf16[1024,128]{1,0:T(8,128)(2,1)}, bf16[512,128]{1,0:T(8,128)(2,1)S(1)}) custom-call(bf16[1024,128]{1,0:T(8,128)(2,1)S(1)} %bitcast.7, f32[512,256]{1,0:T(8,128)S(1)} %shard_map.138.spec_ref, bf16[256,256]{1,0:T(8,128)(2,1)S(1)} %copy-done.8, f32[128,256]{1,0:T(8,128)S(1)} %copy-done.7, bf16[768,256]{1,0:T(8,128)(2,1)S(1)} %copy-done.5, ...), custom_call_target="tpu_custom_call" | custom-call | flops 3000000000 | bytes 2000000 | tf_op jit(solution)/shard_map/pallas_call | solution.py:261
  36.5 8.4 %all-to-all-start.1 = ((bf16[128,8,128]{2,1,0:T(8,128)(2,1)}), bf16[128,8,128]{2,1,0:T(8,128)(2,1)S(1)}, u32[]{:S(2)}, u32[]{:S(2)}) async-start(bf16[128,8,128]{2,1,0:T(8,128)(2,1)} %bitcast.2), calls=%async_computation.1 | async-start | bytes 524288 | tf_op jit(solution)/shard_map/all_to_all | solution.py:227
  44.9 0.0 copy-start
  44.9 0.0 copy-start.1
  44.9 0.0 copy-start.2
  44.9 0.0 copy-start.3
  44.9 12.7 %all-gather = bf16[2048,128]{1,0:T(8,128)(2,1)S(1)} all-gather(bf16[512,128]{1,0:T(8,128)(2,1)S(1)} %get-tuple-element.8), channel_id=2, replica_groups=mesh['seq'=128,'chan'=4] {'chan'}, dimensions={0}, use_global_device_ids=true | all-gather | bytes 655360 | tf_op jit(solution)/shard_map/all_gather | solution.py:280
  57.6 0.0 all-to-all-done.1
  57.6 0.0 copy-done
  57.6 0.0 copy-done.1
  57.6 0.0 copy-done.2
  57.6 0.0 copy-done.3
  57.6 1.1 %shard_map.140 = (bf16[128,512]{1,0:T(8,128)(2,1)}, bf16[128,512]{1,0:T(8,128)(2,1)}, bf16[128,512]{1,0:T(8,128)(2,1)}, bf16[128,512]{1,0:T(8,128)(2,1)}, f32[4,16384]{1,0:T(4,128)}) custom-call(bf16[1024,128]{1,0:T(8,128)(2,1)S(1)} %bitcast.6, bf16[128,512]{1,0:T(8,128)(2,1)S(1)} %copy-done, bf16[128,512]{1,0:T(8,128)(2,1)S(1)} %copy-done.1, ...), custom_call_target="tpu_custom_call" | custom-call | bytes 1572864 | tf_op jit(solution)/shard_map/pallas_call | solution.py:283
Async XLA Ops:
  0.6 21.5 %copy-start.5 = (bf16[768,256]{1,0:T(8,128)(2,1)S(1)}, bf16[768,256]{1,0:T(8,128)(2,1)}, u32[]{:S(2)}) copy-start(bf16[768,256]{1,0:T(8,128)(2,1)} %constant.12.clone.second_ref) | copy-start | bytes 1179652
  2.7 19.4 %copy-start.4 = (f32[4,16384]{1,0:T(4,128)S(1)}, f32[4,16384]{1,0:T(4,128)}, u32[]{:S(2)}) copy-start(f32[4,16384]{1,0:T(4,128)} %filt_ref.1) | copy-start | bytes 786436
  2.7 19.4 %copy-start.7 = (f32[128,256]{1,0:T(8,128)S(1)}, f32[128,256]{1,0:T(8,128)}, u32[]{:S(2)}) copy-start(f32[128,256]{1,0:T(8,128)} %constant.11.clone.twid_ref) | copy-start | bytes 393220
  2.8 19.4 %copy-start.8 = (bf16[256,256]{1,0:T(8,128)(2,1)S(1)}, bf16[256,256]{1,0:T(8,128)(2,1)}, u32[]{:S(2)}) copy-start(bf16[256,256]{1,0:T(8,128)(2,1)} %constant.10.clone.first_ref) | copy-start | bytes 393220
  2.8 31.1 %all-to-all-start = ((bf16[128,8,128]{2,1,0:T(8,128)(2,1)}), bf16[128,8,128]{2,1,0:T(8,128)(2,1)S(1)}, u32[]{:S(2)}, u32[]{:S(2)}) async-start(bf16[128,8,128]{2,1,0:T(8,128)(2,1)} %bitcast.8), calls=%async_computation | async-start | bytes 524288 | tf_op jit(solution)/shard_map/all_to_all | solution.py:227
  22.2 11.7 %copy-start.6 = (bf16[512,256]{1,0:T(8,128)(2,1)S(1)}, bf16[512,256]{1,0:T(8,128)(2,1)}, u32[]{:S(2)}) copy-start(bf16[512,256]{1,0:T(8,128)(2,1)} %constant.13.clone.inverse_ref) | copy-start | bytes 786436
  22.2 11.7 %copy-start.9 = (bf16[128,512]{1,0:T(8,128)(2,1)S(1)}, bf16[128,512]{1,0:T(8,128)(2,1)}, u32[]{:S(2)}) copy-start(bf16[128,512]{1,0:T(8,128)(2,1)} %constant.14.clone.last_ref) | copy-start | bytes 393220
  36.5 21.1 %all-to-all-start.1 = ((bf16[128,8,128]{2,1,0:T(8,128)(2,1)}), bf16[128,8,128]{2,1,0:T(8,128)(2,1)S(1)}, u32[]{:S(2)}, u32[]{:S(2)}) async-start(bf16[128,8,128]{2,1,0:T(8,128)(2,1)} %bitcast.2), calls=%async_computation.1 | async-start | bytes 524288 | tf_op jit(solution)/shard_map/all_to_all | solution.py:227
  44.9 12.8 %copy-start = (bf16[128,512]{1,0:T(8,128)(2,1)S(1)}, bf16[128,512]{1,0:T(8,128)(2,1)}, u32[]{:S(2)}) copy-start(bf16[128,512]{1,0:T(8,128)(2,1)} %outer_ref.3) | copy-start | bytes 393220
  44.9 12.7 %copy-start.1 = (bf16[128,512]{1,0:T(8,128)(2,1)S(1)}, bf16[128,512]{1,0:T(8,128)(2,1)}, u32[]{:S(2)}) copy-start(bf16[128,512]{1,0:T(8,128)(2,1)} %inner_ref.3) | copy-start | bytes 393220
  44.9 12.7 %copy-start.2 = (bf16[128,512]{1,0:T(8,128)(2,1)S(1)}, bf16[128,512]{1,0:T(8,128)(2,1)}, u32[]{:S(2)}) copy-start(bf16[128,512]{1,0:T(8,128)(2,1)} %signal_ref.3) | copy-start | bytes 393220
  44.9 12.7 %copy-start.3 = (bf16[128,512]{1,0:T(8,128)(2,1)S(1)}, bf16[128,512]{1,0:T(8,128)(2,1)}, u32[]{:S(2)}) copy-start(bf16[128,512]{1,0:T(8,128)(2,1)} %cotan_ref.3) | copy-start | bytes 393220

commit v5 on v4

--- a/solution.py
+++ b/solution.py
@@ -17,7 +17,7 @@
 
 
 def member_order(count):
-    flip = count // 2 + count // 4
+    flip = count // 2 + count // 8
     return [r ^ flip for r in range(count)], flip
 
 

time: 59 us -> 58.8 us (level)
  waiting for transfers between devices: 11 us -> 10.3 us
  starting transfers between devices: 27.7 us -> 28.3 us
    all_to_all x2, waiting for transfers between devices: 11 us -> 10.3 us  [exchange(): lax.all_to_all(chunks, 'seq', 0, 0, axis_index_groups=[order], tiled=True)]
    all_to_all x2, starting transfers between devices: 27.7 us -> 28.3 us  [exchange(): lax.all_to_all(chunks, 'seq', 0, 0, axis_index_groups=[order], tiled=True)]
where the time goes in v5:
time: 58.8 us; the launch traced here: 58.5 us
  starting transfers between devices  28.3 us (48%)
  blocking collectives  12.6 us (21%)
  waiting for transfers between devices  10.3 us (18%)
  Pallas kernels  6.44 us (11%)
  between operations  0.8 us (1%)
    all_to_all x2, starting transfers between devices, exchange(): lax.all_to_all(chunks, 'seq', 0, 0, axis_index_groups=[order], tiled=True)  28.3 us
    all_gather x1, blocking collectives, body(): parts = lax.all_gather(corr, 'chan', axis=0, tiled=False)  12.6 us
    all_to_all x2, waiting for transfers between devices, exchange(): lax.all_to_all(chunks, 'seq', 0, 0, axis_index_groups=[order], tiled=True)  10.3 us
    pallas_call x1, Pallas kernels, body(): call(conv_kernel, (jax.ShapeDtypeStruct((wide, cols), BF), jax.ShapeDtype...  2.6 us
    pallas_call x1, Pallas kernels, body(): call(functools.partial(pack_kernel, flip), jax.ShapeDtypeStruct((wide, co...  2.08 us
  transfers between devices with their start and end apart: 2, of which 1 were waited for; matrix products, arithmetic and copies ran while one was open for 0% of the time, Pallas kernels for 1%

profile of v5, /device:TPU:1, one launch (start us, length us, event | category | flops | bytes accessed | tf_op | source)
XLA Modules:
  0.0 58.5 jit_solution(9526419970709787492)
XLA Ops:
  0.6 0.0 copy-start.5
  0.6 2.1 %shard_map.137 = bf16[1024,128]{1,0:T(8,128)(2,1)} custom-call(bf16[128,512]{1,0:T(8,128)(2,1)} %outer_ref.3, bf16[128,512]{1,0:T(8,128)(2,1)} %inner_ref.3, bf16[128,512]{1,0:T(8,128)(2,1)} %signal_ref.3, bf16[128,512]{1,0:T(8,128)(2,1)} %cotan_ref.3), custom_call_target="tpu_custom_call" | custom-call | bytes 786432 | tf_op jit(solution)/shard_map/pallas_call | solution.py:241
  2.7 0.0 copy-start.4
  2.7 0.0 copy-start.7
  2.8 0.0 copy-start.8
  2.8 19.2 %all-to-all-start = ((bf16[128,8,128]{2,1,0:T(8,128)(2,1)}), bf16[128,8,128]{2,1,0:T(8,128)(2,1)S(1)}, u32[]{:S(2)}, u32[]{:S(2)}) async-start(bf16[128,8,128]{2,1,0:T(8,128)(2,1)} %bitcast.8), calls=%async_computation | async-start | bytes 524288 | tf_op jit(solution)/shard_map/all_to_all | solution.py:227
  22.0 0.0 copy-done.5
  22.0 0.0 copy-done.4
  22.0 0.0 copy-done.7
  22.1 0.0 copy-done.8
  22.1 0.0 copy-start.6
  22.1 0.0 copy-start.9
  22.1 0.7 %shard_map.138.spec_ref = f32[512,256]{1,0:T(8,128)S(1)} custom-call(f32[4,16384]{1,0:T(4,128)S(1)} %copy-done.4, bf16[256,256]{1,0:T(8,128)(2,1)S(1)} %copy-done.8, f32[128,256]{1,0:T(8,128)S(1)} %copy-done.7, bf16[768,256]{1,0:T(8,128)(2,1)S(1)} %copy-done.5), custom_call_target="tpu_custom_call" | custom-call | flops 1000000000 | bytes 1000000 | tf_op jit(solution)/shard_map/pallas_call | solution.py:255
  22.8 10.3 %all-to-all-done = bf16[128,8,128]{2,1,0:T(8,128)(2,1)S(1)} async-done(((bf16[128,8,128]{2,1,0:T(8,128)(2,1)}), bf16[128,8,128]{2,1,0:T(8,128)(2,1)S(1)}, u32[]{:S(2)}, u32[]{:S(2)}) %all-to-all-start) | async-done | bytes 262176 | tf_op jit(solution)/shard_map/all_to_all | solution.py:227
  33.0 0.0 copy-done.6
  33.0 0.0 copy-done.9
  33.0 2.6 %shard_map.139 = (bf16[1024,128]{1,0:T(8,128)(2,1)}, bf16[512,128]{1,0:T(8,128)(2,1)S(1)}) custom-call(bf16[1024,128]{1,0:T(8,128)(2,1)S(1)} %bitcast.7, f32[512,256]{1,0:T(8,128)S(1)} %shard_map.138.spec_ref, bf16[256,256]{1,0:T(8,128)(2,1)S(1)} %copy-done.8, f32[128,256]{1,0:T(8,128)S(1)} %copy-done.7, bf16[768,256]{1,0:T(8,128)(2,1)S(1)} %copy-done.5, ...), custom_call_target="tpu_custom_call" | custom-call | flops 3000000000 | bytes 2000000 | tf_op jit(solution)/shard_map/pallas_call | solution.py:261
  35.6 9.1 %all-to-all-start.1 = ((bf16[128,8,128]{2,1,0:T(8,128)(2,1)}), bf16[128,8,128]{2,1,0:T(8,128)(2,1)S(1)}, u32[]{:S(2)}, u32[]{:S(2)}) async-start(bf16[128,8,128]{2,1,0:T(8,128)(2,1)} %bitcast.2), calls=%async_computation.1 | async-start | bytes 524288 | tf_op jit(solution)/shard_map/all_to_all | solution.py:227
  44.7 0.0 copy-start
  44.8 0.0 copy-start.1
  44.8 0.0 copy-start.2
  44.8 0.0 copy-start.3
  44.8 12.6 %all-gather = bf16[2048,128]{1,0:T(8,128)(2,1)S(1)} all-gather(bf16[512,128]{1,0:T(8,128)(2,1)S(1)} %get-tuple-element.8), channel_id=2, replica_groups=mesh['seq'=128,'chan'=4] {'chan'}, dimensions={0}, use_global_device_ids=true | all-gather | bytes 655360 | tf_op jit(solution)/shard_map/all_gather | solution.py:280
  57.4 0.0 all-to-all-done.1
  57.4 0.0 copy-done
  57.4 0.0 copy-done.1
  57.4 0.0 copy-done.2
  57.4 0.0 copy-done.3
  57.4 1.1 %shard_map.140 = (bf16[128,512]{1,0:T(8,128)(2,1)}, bf16[128,512]{1,0:T(8,128)(2,1)}, bf16[128,512]{1,0:T(8,128)(2,1)}, bf16[128,512]{1,0:T(8,128)(2,1)}, f32[4,16384]{1,0:T(4,128)}) custom-call(bf16[1024,128]{1,0:T(8,128)(2,1)S(1)} %bitcast.6, bf16[128,512]{1,0:T(8,128)(2,1)S(1)} %copy-done, bf16[128,512]{1,0:T(8,128)(2,1)S(1)} %copy-done.1, ...), custom_call_target="tpu_custom_call" | custom-call | bytes 1572864 | tf_op jit(solution)/shard_map/pallas_call | solution.py:283
Async XLA Ops:
  0.6 21.4 %copy-start.5 = (bf16[768,256]{1,0:T(8,128)(2,1)S(1)}, bf16[768,256]{1,0:T(8,128)(2,1)}, u32[]{:S(2)}) copy-start(bf16[768,256]{1,0:T(8,128)(2,1)} %constant.12.clone.second_ref) | copy-start | bytes 1179652
  2.7 19.3 %copy-start.4 = (f32[4,16384]{1,0:T(4,128)S(1)}, f32[4,16384]{1,0:T(4,128)}, u32[]{:S(2)}) copy-start(f32[4,16384]{1,0:T(4,128)} %filt_ref.1) | copy-start | bytes 786436
  2.7 19.3 %copy-start.7 = (f32[128,256]{1,0:T(8,128)S(1)}, f32[128,256]{1,0:T(8,128)}, u32[]{:S(2)}) copy-start(f32[128,256]{1,0:T(8,128)} %constant.11.clone.twid_ref) | copy-start | bytes 393220
  2.8 19.3 %copy-start.8 = (bf16[256,256]{1,0:T(8,128)(2,1)S(1)}, bf16[256,256]{1,0:T(8,128)(2,1)}, u32[]{:S(2)}) copy-start(bf16[256,256]{1,0:T(8,128)(2,1)} %constant.10.clone.first_ref) | copy-start | bytes 393220
  2.8 30.3 %all-to-all-start = ((bf16[128,8,128]{2,1,0:T(8,128)(2,1)}), bf16[128,8,128]{2,1,0:T(8,128)(2,1)S(1)}, u32[]{:S(2)}, u32[]{:S(2)}) async-start(bf16[128,8,128]{2,1,0:T(8,128)(2,1)} %bitcast.8), calls=%async_computation | async-start | bytes 524288 | tf_op jit(solution)/shard_map/all_to_all | solution.py:227
  22.1 11.0 %copy-start.6 = (bf16[512,256]{1,0:T(8,128)(2,1)S(1)}, bf16[512,256]{1,0:T(8,128)(2,1)}, u32[]{:S(2)}) copy-start(bf16[512,256]{1,0:T(8,128)(2,1)} %constant.13.clone.inverse_ref) | copy-start | bytes 786436
  22.1 11.0 %copy-start.9 = (bf16[128,512]{1,0:T(8,128)(2,1)S(1)}, bf16[128,512]{1,0:T(8,128)(2,1)}, u32[]{:S(2)}) copy-start(bf16[128,512]{1,0:T(8,128)(2,1)} %constant.14.clone.last_ref) | copy-start | bytes 393220
  35.6 21.7 %all-to-all-start.1 = ((bf16[128,8,128]{2,1,0:T(8,128)(2,1)}), bf16[128,8,128]{2,1,0:T(8,128)(2,1)S(1)}, u32[]{:S(2)}, u32[]{:S(2)}) async-start(bf16[128,8,128]{2,1,0:T(8,128)(2,1)} %bitcast.2), calls=%async_computation.1 | async-start | bytes 524288 | tf_op jit(solution)/shard_map/all_to_all | solution.py:227
  44.7 12.6 %copy-start = (bf16[128,512]{1,0:T(8,128)(2,1)S(1)}, bf16[128,512]{1,0:T(8,128)(2,1)}, u32[]{:S(2)}) copy-start(bf16[128,512]{1,0:T(8,128)(2,1)} %outer_ref.3) | copy-start | bytes 393220
  44.8 12.6 %copy-start.1 = (bf16[128,512]{1,0:T(8,128)(2,1)S(1)}, bf16[128,512]{1,0:T(8,128)(2,1)}, u32[]{:S(2)}) copy-start(bf16[128,512]{1,0:T(8,128)(2,1)} %inner_ref.3) | copy-start | bytes 393220
  44.8 12.6 %copy-start.2 = (bf16[128,512]{1,0:T(8,128)(2,1)S(1)}, bf16[128,512]{1,0:T(8,128)(2,1)}, u32[]{:S(2)}) copy-start(bf16[128,512]{1,0:T(8,128)(2,1)} %signal_ref.3) | copy-start | bytes 393220
  44.8 12.6 %copy-start.3 = (bf16[128,512]{1,0:T(8,128)(2,1)S(1)}, bf16[128,512]{1,0:T(8,128)(2,1)}, u32[]{:S(2)}) copy-start(bf16[128,512]{1,0:T(8,128)(2,1)} %cotan_ref.3) | copy-start | bytes 393220
